TPU v7x, 32 devices: a whole 2x2x4 slice. The times are simulated.
32 devices in a mesh: dp: 8 (over z, x), sub: 4 (over y, core).
Axes of the slice: x: 2, y: 2, z: 4, core: 2. Of those that a mesh axis runs over, the one named last changes fastest.
Arguments:
- tokens: bfloat16 [32768, 512], P(('dp', 'sub')), may hold values from -6 to 6
- cotangent: bfloat16 [32768, 512], P(('dp', 'sub')), may hold values from -6 to 6
- item_lengths: int32 [32, 8], P(('dp', 'sub')), may hold values from 0 to 1024, as said below
- joint_weight: bfloat16 [512, 1536], P(('dp', 'sub')), may hold values from -0.25 to 0.25
- output_weight: bfloat16 [512, 512], P(('dp', 'sub')), may hold values from -1.5 to 1.5
- expand_weight: bfloat16 [512, 2048], P(('dp', 'sub')), may hold values from -0.25 to 0.25
- reduce_weight: bfloat16 [2048, 512], P(('dp', 'sub')), may hold values from -0.125 to 0.125
- attn_gain: bfloat16 [512], P(('dp', 'sub')), may hold values from 0.099609375 to 1.8984375
- attn_shift: bfloat16 [512], P(('dp', 'sub')), may hold values from -3 to 3
- ffn_gain: bfloat16 [512], P(('dp', 'sub')), may hold values from 0.099609375 to 1.8984375
- ffn_shift: bfloat16 [512], P(('dp', 'sub')), may hold values from -3 to 3
- expand_bias: bfloat16 [2048], P(('dp', 'sub')), may hold values from -3 to 3
- reduce_bias: bfloat16 [512], P(('dp', 'sub')), may hold values from -3 to 3
Outputs:
- mixed: bfloat16 [32768, 512], P(('dp', 'sub'))
- token_grad: bfloat16 [32768, 512], P(('dp', 'sub'))
- joint_grad: float32 [512, 1536], P(('dp', 'sub'))
- output_grad: float32 [512, 512], P(('dp', 'sub'))
- expand_grad: float32 [512, 2048], P(('dp', 'sub'))
- reduce_grad: float32 [2048, 512], P(('dp', 'sub'))
- attn_gain_grad: float32 [512], P(('dp', 'sub'))
- attn_shift_grad: float32 [512], P(('dp', 'sub'))
- ffn_gain_grad: float32 [512], P(('dp', 'sub'))
- ffn_shift_grad: float32 [512], P(('dp', 'sub'))
- expand_bias_grad: float32 [2048], P(('dp', 'sub'))
- reduce_bias_grad: float32 [512], P(('dp', 'sub'))
Inputs may be any that keep to these rules, and one draw needn't show every extreme that they name: item_lengths[d, i] is the length of item i of device d, 0 for an empty slot; nonzero lengths are 64 or more; a device's items, each rounded up to a multiple of 16, fit in its 1024 slots; device 0's first item has 1024 tokens.
All inputs are finite; a program needn't handle non-finite values.
Results may differ from a plain program's by a relative error of at most 0.011.
Values may be sent and summed in bfloat16 or wider, within the bound.
No kernel may reach another device: no remote copies, remote signals or barrier semaphores. Data moves between devices by JAX's collectives and lax.ppermute only.
A program may use at most 256 MiB of HBM per device.

v0:
```python
import functools
import math

import jax
import jax.numpy as jnp
import numpy as np
from jax import lax
from jax.experimental import pallas as pl
from jax.experimental.pallas import tpu as pltpu
from jax.sharding import PartitionSpec as P

HEADS = 8
BLOCK = 16
LEVELS = 7
TILE = 64
POOL = 128
GROUPS = 2
DIM = 64
STEP = 8
LOG_TWO = math.log(2.0)
NEGATIVE = -1e30
ROOT_HALF = 1.0 / math.sqrt(2.0)
DENSITY = 1.0 / math.sqrt(2.0 * math.pi)
AXES = ("dp", "sub")
BF = jnp.bfloat16
F32 = jnp.float32
MIB = 1 << 20


class Level:
    def __init__(self, level, seq, base):
        self.level = level
        self.factor = 1 << level
        self.count = seq // self.factor
        self.width = BLOCK * self.factor
        self.blocks = seq // self.width
        self.pad = BLOCK if self.blocks > 2 else 0
        self.base = base
        self.rows = self.count + 2 * self.pad

    def pieces(self, tile):
        if self.width < TILE:
            return [(tile * (TILE // self.factor), TILE // self.factor + 2 * BLOCK)]
        block = tile // (self.width // TILE)
        if self.blocks > 2:
            return [(block * BLOCK, BLOCK), ((block + 2) * BLOCK, BLOCK)]
        return [((self.blocks - 1 - block) * BLOCK, BLOCK)]

    def spans(self, tile):
        return [(pl.multiple_of(self.base + first, BLOCK), n) for first, n in self.pieces(tile)]


def geometry(seq):
    levels, base = [], 0
    for level in range(LEVELS):
        levels.append(Level(level, seq, base))
        base += levels[-1].rows
    return levels, base, sum(n for v in levels for _, n in v.pieces(0))


def split_levels(seq):
    levels, _, _ = geometry(seq)
    near = [v for v in levels[1:] if v.width <= POOL]
    far = [v for v in levels[1:] if v.width > POOL]
    return near, far, far[0].base


def spreading(seq):
    levels, total, _ = geometry(seq)
    near, far, far_base = split_levels(seq)
    near_rows = sum(POOL // v.factor for v in near)
    spread = np.zeros((seq, near_rows + total - far_base), np.float32)
    at = 0
    for v in near:
        for t in range(seq):
            spread[t, at + t % POOL // v.factor] = 1.0 / v.factor
        at += POOL // v.factor
    for v in far:
        for t in range(seq):
            spread[t, near_rows + v.base - far_base + v.pad + t // v.factor] = 1.0 / v.factor
    return spread


class Order:
    def __init__(self, devices, turned=False):
        self.devices = devices
        self.bits = [1 << k for k in reversed(range(devices.bit_length() - 1))]
        self.stepped = devices == 32
        if not turned:
            self.turned = Order(devices, True)
        elif self.stepped:
            self.bits[-3:-1] = self.bits[-2], self.bits[-3]

    def flip(self, p):
        value = 0
        for k, bit in enumerate(self.bits):
            value = value + ((p >> k) & 1) * bit
        return value


def dot(left, right, contract=(1, 0)):
    return lax.dot_general(
        left, right, (((contract[0],), (contract[1],)), ((), ())), preferred_element_type=F32
    )


def iota(shape, axis):
    return lax.broadcasted_iota(jnp.int32, shape, axis)


def unpack_rows(order, me, halves, columns, target, chunk, places=slice(None)):
    rows = halves[0].shape[0]
    if not order.stepped:
        target[:rows, places] = halves[0][:, columns]
        target[rows:, places] = halves[1][:, columns]
        return
    for p in range(order.devices):
        half, at = divmod(p * chunk, rows)
        row = pl.multiple_of((me ^ order.flip(p)) * chunk, chunk)
        target[pl.ds(row, chunk), places] = halves[half][at : at + chunk, columns]


def pack_rows(order, me, source, halves, columns, chunk):
    rows = halves[0].shape[0]
    if not order.stepped:
        halves[0][:, columns] = source[:rows]
        halves[1][:, columns] = source[rows:]
        return
    for p in range(order.devices):
        half, at = divmod(p * chunk, rows)
        row = pl.multiple_of((me ^ order.flip(p)) * chunk, chunk)
        halves[half][at : at + chunk, columns] = source[pl.ds(row, chunk), :]


def owners(order, me, shape):
    return me ^ order.flip(iota(shape, 0))


def spread_lanes(order, me, halves, columns, row, offset, chunk, total):
    n = order.devices
    block = jnp.concatenate([half[:, columns] for half in halves], axis=0)
    step = block.shape[0] // n
    pick = (iota((n, block.shape[0]), 1) == iota((n, block.shape[0]), 0) * step + row).astype(BF)
    rows = dot(pick, block).astype(BF)
    lanes = block.shape[1]
    place = (iota((lanes, total), 0) == iota((lanes, total), 1) % chunk + offset).astype(BF)
    wide = dot(rows, place)
    mine = iota((n, total), 1) // chunk == owners(order, me, (n, total))
    return jnp.sum(jnp.where(mine, wide, 0.0), axis=0, keepdims=True)


def fold_lanes(order, me, vector, offset, chunk, lanes):
    n, total = order.devices, vector.shape[1]
    mine = iota((n, total), 1) // chunk == owners(order, me, (n, total))
    wide = jnp.where(mine, vector, 0.0).astype(BF)
    place = (iota((total, lanes), 1) == iota((total, lanes), 0) % chunk + offset).astype(BF)
    return dot(wide, place)


def place_rows(rows, row, step):
    n = rows.shape[0]
    pick = (iota((n * step, n), 0) == iota((n * step, n), 1) * step + row).astype(BF)
    return dot(pick, rows.astype(BF))


def live_column(lens, first, rows):
    position = first + iota((rows, 1), 0)
    start, live = 0, jnp.zeros((rows, 1), jnp.bool_)
    for i in range(lens.shape[1]):
        length = lens[0, i]
        live = live | ((position >= start) & (position < start + length))
        start = start + (length + BLOCK - 1) // BLOCK * BLOCK
    return live


def tile_bias(lens, tile, levels, copies):
    position = tile * TILE + iota((1, copies * TILE), 1) % TILE
    low, high, start = position, position + 1, 0
    for i in range(lens.shape[1]):
        length = lens[0, i]
        inside = (position >= start) & (position < start + length)
        low = jnp.where(inside, start, low)
        high = jnp.where(inside, start + length, high)
        start = start + (length + BLOCK - 1) // BLOCK * BLOCK
    parts = []
    for v in levels:
        reach = (position // v.width - 1) * v.width
        least = jnp.maximum(low, reach)
        most = jnp.minimum(high - v.factor, reach + 3 * v.width - 1)
        half = v.width // 2
        lower = (position // half - 1) * half
        for first, rows in v.pieces(tile):
            begin = (first - v.pad + iota((rows, copies * TILE), 0)) * v.factor
            valid = (begin >= least) & (begin <= most)
            if v.level > 0:
                valid = valid & ((begin < lower) | (begin >= lower + 3 * half))
            parts.append(jnp.where(valid, v.level * LOG_TWO, NEGATIVE))
    return jnp.concatenate(parts, axis=0)


def window_of(ref, tile, levels):
    return jnp.concatenate([ref[pl.ds(at, n), :] for v in levels for at, n in v.spans(tile)], axis=0)


def split_heads(rows):
    head = iota(rows.shape, 1) // DIM
    zero = jnp.zeros_like(rows)
    return jnp.concatenate([jnp.where(head == h, rows, zero) for h in range(rows.shape[1] // DIM)], axis=0)


def own_heads(full):
    heads = full.shape[1] // DIM
    head = iota((TILE, full.shape[1]), 1) // DIM
    own = full[:TILE]
    for h in range(1, heads):
        own = jnp.where(head == h, full[h * TILE : (h + 1) * TILE], own)
    return own


def normalize(values):
    centre = values - jnp.mean(values, axis=-1, keepdims=True)
    scale = lax.rsqrt(jnp.mean(centre * centre, axis=-1, keepdims=True) + 1e-05)
    return centre * scale, scale


def norm_back(grad, normed, scale, gain):
    scaled = grad * gain
    return scale * (
        scaled
        - jnp.mean(scaled, axis=-1, keepdims=True)
        - normed * jnp.mean(scaled * normed, axis=-1, keepdims=True)
    )


def prepare_kernel(seq, lens_ref, bias_ref):
    levels, _, _ = geometry(seq)
    step = pl.program_id(0)
    for t in range(STEP):
        bias_ref[t] = tile_bias(lens_ref, step * STEP + t, levels, bias_ref.shape[2] // TILE)


def means(seq, fine_ref, wide_ref):
    near, far, far_base = split_levels(seq)
    at = 0
    for v in near:
        n = POOL // v.factor
        same = iota((n, POOL), 1) // v.factor == iota((n, POOL), 0)
        fine_ref[at : at + n, :] = jnp.where(same, 1.0 / v.factor, 0.0).astype(BF)
        at += n
    for v in far:
        same = iota((v.rows, seq), 1) // v.factor == iota((v.rows, seq), 0) - v.pad
        base = v.base - far_base
        wide_ref[base : base + v.rows, :] = jnp.where(same, 1.0 / v.factor, 0.0).astype(BF)


def attend_kernel(order, seq, group, me_ref, bias_ref, x_ref, *refs):
    first_group = group == 0
    if first_group:
        lo_ref, hi_ref, vec_ref = refs[:3]
        p_ref, ctx_ref, q_ref, kx_ref, vx_ref, in_ref, w_ref, gain_ref = refs[3:11]
        fine_ref, wide_ref = refs[11:]
    else:
        w_ref, p_ref, ctx_ref, q_ref, kx_ref, vx_ref, fine_ref, wide_ref = refs
    levels, total, _ = geometry(seq)
    near, _, far_base = split_levels(seq)
    tile = pl.program_id(0)
    lanes = q_ref.shape[1]
    me = me_ref[0]

    @pl.when(tile == 0)
    def _():
        d = x_ref.shape[1]
        means(seq, fine_ref, wide_ref)
        if first_group:
            chunk = d // order.devices
            unpack_rows(order, me, (lo_ref, hi_ref), slice(0, 3 * d), w_ref, chunk)
            if order.stepped:
                tail = slice(3 * d, 3 * d + 128)
                gain = spread_lanes(order, me, (lo_ref, hi_ref), tail, 0, 0, chunk, d)
                shift = spread_lanes(order, me, (lo_ref, hi_ref), tail, 0, chunk, chunk, d)
            else:
                gain, shift = vec_ref[0:1, :], vec_ref[1:2, :]
            gain_ref[...] = jnp.broadcast_to(gain, gain_ref.shape)
        kx_ref[...] = jnp.zeros_like(kx_ref)
        vx_ref[...] = jnp.zeros_like(vx_ref)
        step = 256
        pad = levels[0].pad
        for r in range(0, seq, step):
            if first_group:
                hat, _ = normalize(x_ref[r : r + step, :].astype(F32))
                first_in = (hat * gain + shift).astype(BF)
                in_ref[r : r + step, :] = first_in
            else:
                first_in = x_ref[r : r + step, :]
            query, keys, vals = [
                dot(first_in, w_ref[:, k * d + group * lanes : k * d + (group + 1) * lanes]).astype(BF)
                for k in range(3)
            ]
            q_ref[r : r + step, :] = query * jnp.asarray(0.125, BF)
            kx_ref[pad + r : pad + r + step, :] = keys
            vx_ref[pad + r : pad + r + step, :] = vals
        for ref in (kx_ref, vx_ref):
            for t in range(seq // POOL):
                rows = ref[pad + t * POOL : pad + (t + 1) * POOL, :]
                pooled = dot(fine_ref[...], rows).astype(BF)
                at = 0
                for v in near:
                    n = POOL // v.factor
                    ref[v.base + v.pad + t * n : v.base + v.pad + (t + 1) * n, :] = pooled[at : at + n]
                    at += n
            ref[far_base:total, :] = dot(wide_ref[...], ref[pad : pad + seq, :]).astype(BF)

    tiles = range(STEP)
    scores = []
    for t in tiles:
        at = tile * STEP + t
        query = split_heads(q_ref[pl.ds(pl.multiple_of(at * TILE, TILE), TILE), :])
        scores.append(dot(window_of(kx_ref, at, levels), query, (1, 1)))
    probs = []
    for t in tiles:
        bias = jnp.concatenate([bias_ref[t]] * (scores[t].shape[1] // bias_ref.shape[2]), axis=1)
        score = scores[t] + bias
        peak = jnp.max(score, axis=0, keepdims=True)
        weight = jnp.exp(score - peak)
        share = 1.0 / jnp.sum(weight, axis=0, keepdims=True)
        probs.append((weight * share).astype(BF))
        p_ref[t] = probs[t]
    for t in tiles:
        context = dot(probs[t], window_of(vx_ref, tile * STEP + t, levels), (0, 0))
        ctx_ref[t * TILE : (t + 1) * TILE, :] = own_heads(context).astype(BF)


def ffn_block(rows, in_ref, og_ref, act_scr, eg_scr, mix_ref, sg_ref, we, wr, bias):
    for r in range(0, in_ref.shape[0], rows):
        part = slice(r, r + rows)
        expanded = dot(in_ref[part, :], we[...]) + bias
        phi = 0.5 * (1.0 + lax.erf(expanded * ROOT_HALF))
        activated = (expanded * phi).astype(BF)
        act_scr[part, :] = activated
        slope = phi + expanded * (jnp.exp(-0.5 * expanded * expanded) * DENSITY)
        expanded_grad = (dot(og_ref[part, :], wr[...], (1, 1)) * slope).astype(BF)
        eg_scr[part, :] = expanded_grad
        mix_ref[part, :] += dot(activated, wr[...])
        sg_ref[part, :] += dot(expanded_grad, we[...], (1, 1))


def ffn_kernel(order, part, me_ref, lens_ref, *refs):
    first = part == 0
    if first:
        x_ref, cot_ref, ctx0_ref, ctx1_ref, lo1_ref, hi1_ref, vec_ref, ebias_ref = refs[:8]
        hidden_ref, in_ref, og_ref, mix_ref, sg_ref, esum_ref, lo_ref, hi_ref = refs[8:16]
        own = (lo1_ref, hi1_ref)
        we_scr, wr_scr, wo_scr, eb_scr, in_scr, act_scr, eg_scr, grad_scr, vec_scr = refs[16:]
    else:
        cot_ref, hidden_ref, in_ref, og_ref, _, _, esum0_ref, ctx0_ref, ctx1_ref = refs[:9]
        lo1_ref, hi1_ref, lo2_ref, hi2_ref, vec_ref, ebias_ref = refs[9:15]
        mixed_ref, hg_ref, cg_ref, lo_ref, hi_ref, olo_ref, ohi_ref, sums_ref, esum_ref, mix_ref, sg_ref = refs[15:26]
        own = (lo2_ref, hi2_ref)
        we_scr, wr_scr, wo_scr, eb_scr, in_scr, act_scr, eg_scr, grad_scr, vec_scr, branch_scr = refs[26:]
    step = pl.program_id(0)
    me = me_ref[0]
    seq, d = cot_ref.shape
    rows = 512
    chunk = d // order.devices
    wide = 2 * d
    shared = (lo1_ref, hi1_ref)
    turned = order.turned
    half = ctx0_ref.shape[1]
    tail = slice(5 * d, 5 * d + 128)

    def bias_of(block, at):
        if order.stepped:
            return spread_lanes(order, me, shared, tail, 1, block * chunk, chunk, d)
        return ebias_ref[:, at : at + d]

    def live_rows(span):
        return live_column(lens_ref, span.start, rows).astype(F32)

    def open_rows(span):
        live = live_rows(span)
        out = dot(ctx0_ref[span, :], wo_scr[:half, :]) + dot(ctx1_ref[span, :], wo_scr[half:, :])
        hidden = x_ref[span, :].astype(F32) + live * out
        hidden_ref[span, :] = hidden
        hat, _ = normalize(hidden)
        in_ref[span, :] = (hat * vec_scr[0:1, :] + vec_scr[1:2, :]).astype(BF)
        og_ref[span, :] = (cot_ref[span, :].astype(F32) * live).astype(BF)

    def close_rows(span):
        live = live_rows(span)
        hidden = hidden_ref[span, :]
        mixed_ref[span, :] = (hidden + live * (mix_ref[span, :] + vec_scr[1:2, :])).astype(BF)
        hat, scale = normalize(hidden)
        second_grad = sg_ref[span, :]
        sums_ref[0:1, :] += jnp.sum(second_grad * hat, axis=0, keepdims=True)
        sums_ref[1:2, :] += jnp.sum(second_grad, axis=0, keepdims=True)
        sums_ref[2:3, :] += jnp.sum(og_ref[span, :].astype(F32), axis=0, keepdims=True)
        grad = cot_ref[span, :].astype(F32) + norm_back(second_grad, hat, scale, vec_scr[0:1, :])
        hg_ref[span, :] = grad
        branch = (grad * live).astype(BF)
        branch_scr[span, :] = branch
        cg_ref[span, :] = dot(branch, wo_scr[...], (1, 1)).astype(BF)

    @pl.when(step == 0)
    def _():
        unpack_rows(order, me, own, slice(0, wide), we_scr, chunk)
        unpack_rows(order, me, own, slice(wide, 2 * wide), wr_scr, chunk)
        unpack_rows(order, me, shared, slice(2 * wide, 2 * wide + d), wo_scr, chunk)
        for k in range(2):
            block = 2 * part + k
            eb_scr[:, k * d : (k + 1) * d] = bias_of(block, block * d)
        if first:
            if order.stepped:
                gain = spread_lanes(order, me, shared, tail, 0, 0, chunk, d)
                shift = spread_lanes(order, me, shared, tail, 0, chunk, chunk, d)
            else:
                gain, shift = vec_ref[2:3, :], vec_ref[3:4, :]
            vec_scr[0:1, :] = gain
            vec_scr[1:2, :] = shift
            mix_ref[...] = jnp.zeros_like(mix_ref)
            sg_ref[...] = jnp.zeros_like(sg_ref)
        else:
            in_scr[...] = in_ref[...].T
            if order.stepped:
                vec_scr[0:1, :] = spread_lanes(order, me, shared, tail, 0, 0, chunk, d)
                vec_scr[1:2, :] = spread_lanes(order, me, shared, tail, 0, 2 * chunk, chunk, d)
            else:
                vec_scr[0:1, :] = vec_ref[2:3, :]
                vec_scr[1:2, :] = vec_ref[4:5, :]
            sums_ref[...] = jnp.zeros_like(sums_ref)
        if first:
            for r in range(0, seq, rows):
                open_rows(slice(r, r + rows))
            in_scr[...] = in_ref[...].T

    now = pl.ds(pl.multiple_of(step * d, d), d)
    ffn_block(
        rows, in_ref, og_ref, act_scr, eg_scr, mix_ref, sg_ref, we_scr.at[:, now], wr_scr.at[:, now], eb_scr[:, now]
    )
    esum_ref[:, now] = jnp.sum(eg_scr[...].astype(F32), axis=0, keepdims=True)
    mine = order if first else turned
    grad_scr[...] = dot(in_scr[...], eg_scr[...]).astype(BF)
    pack_rows(mine, me, grad_scr, (lo_ref, hi_ref), now, chunk)
    grad_scr[...] = dot(act_scr[...], og_ref[...], (0, 0)).astype(BF)
    pack_rows(mine, me, grad_scr, (lo_ref, hi_ref), pl.ds(pl.multiple_of(wide + step * d, d), d), chunk)

    if first:
        return

    @pl.when(step == pl.num_programs(0) - 1)
    def _():
        for r in range(0, seq, rows):
            close_rows(slice(r, r + rows))
        grad_scr[:half, :] = dot(ctx0_ref[...], branch_scr[...], (0, 0)).astype(BF)
        grad_scr[half:, :] = dot(ctx1_ref[...], branch_scr[...], (0, 0)).astype(BF)
        pack_rows(order, me, grad_scr, (olo_ref, ohi_ref), slice(0, d), chunk)
        if order.stepped:
            small = jnp.zeros((order.devices, 128), F32)
            for k in range(3):
                small += fold_lanes(order, me, sums_ref[k : k + 1, :], k * chunk, chunk, 128)
            more = jnp.zeros((order.devices, 128), F32)
            for k in range(2):
                now = slice(k * d, (k + 1) * d)
                more += fold_lanes(order, me, esum0_ref[:, now], k * chunk, chunk, 128)
                more += fold_lanes(order, me, esum_ref[:, now], (2 + k) * chunk, chunk, 128)
            block = (place_rows(small, 0, chunk) + place_rows(more, 1, chunk)).astype(BF)
            olo_ref[:, d:] = block[: d // 2]
            ohi_ref[:, d:] = block[d // 2 :]


def attend_back_kernel(
    order,
    seq,
    group,
    me_ref,
    p_ref,
    q_ref,
    cg_ref,
    kx_ref,
    vx_ref,
    in_ref,
    w_ref,
    spread_ref,
    *refs,
):
    last = group == GROUPS - 1
    if last:
        x_ref, fig0_ref, hg_ref, gain_ref, lo_ref, hi_ref, tg_ref, sums_ref = refs[:8]
        dk_scr, dv_scr, dj_scr, j_scr = refs[8:]
    else:
        olo_ref, ohi_ref, lo_ref, hi_ref, fig_ref = refs[:5]
        dk_scr, dv_scr, dj_scr, j_scr = refs[5:]
    d = in_ref.shape[1]
    chunk = d // order.devices
    levels, total, _ = geometry(seq)
    near, _, far_base = split_levels(seq)
    tile = pl.program_id(0)
    lanes = q_ref.shape[1]
    me = me_ref[0]

    @pl.when(tile == 0)
    def _():
        dk_scr[...] = jnp.zeros_like(dk_scr)
        dv_scr[...] = jnp.zeros_like(dv_scr)
        if not last:
            lo_ref[:, 3 * lanes :] = olo_ref[...]
            hi_ref[:, 3 * lanes :] = ohi_ref[...]

    tiles = range(STEP)
    grads, prob_grads, score_grads = [], [], []
    for t in tiles:
        grads.append(split_heads(cg_ref[t * TILE : (t + 1) * TILE, :]))
        prob_grads.append(dot(window_of(vx_ref, tile * STEP + t, levels), grads[t], (1, 1)))
    for t in tiles:
        prob = p_ref[t].astype(F32)
        inner = jnp.sum(prob * prob_grads[t], axis=0, keepdims=True)
        score_grads.append((prob * (prob_grads[t] - inner)).astype(BF))
    for t in tiles:
        now = tile * STEP + t
        query_grad = own_heads(dot(score_grads[t], window_of(kx_ref, now, levels), (0, 0)))
        dj_scr[pl.ds(pl.multiple_of(now * TILE, TILE), TILE), :lanes] = (query_grad * 0.125).astype(BF)
    for t in tiles:
        now = tile * STEP + t
        key_grad = dot(score_grads[t], split_heads(q_ref[t * TILE : (t + 1) * TILE, :]))
        val_grad = dot(p_ref[t], grads[t])
        at = 0
        for v in levels:
            for row, n in v.spans(now):
                dk_scr[pl.ds(row, n), :] += key_grad[at : at + n]
                dv_scr[pl.ds(row, n), :] += val_grad[at : at + n]
                at += n

    @pl.when(tile == pl.num_programs(0) - 1)
    def _():
        pad = levels[0].pad
        for ref, at in ((dk_scr, lanes), (dv_scr, 2 * lanes)):
            far = ref[far_base:total, :].astype(BF)
            for t in range(seq // POOL):
                parts = []
                for v in near:
                    n = POOL // v.factor
                    base = v.base + v.pad + t * n
                    parts.append(ref[base : base + n, :].astype(BF))
                parts.append(far)
                spread = dot(spread_ref[t * POOL : (t + 1) * POOL, :], jnp.concatenate(parts, axis=0))
                whole = ref[pad + t * POOL : pad + (t + 1) * POOL, :] + spread
                dj_scr[t * POOL : (t + 1) * POOL, at : at + lanes] = whole.astype(BF)
        j_scr[...] = dot(in_ref[...], dj_scr[...], (0, 0)).astype(BF)
        mine = order.turned if last else order
        pack_rows(mine, me, j_scr, (lo_ref, hi_ref), slice(0, 3 * lanes), chunk)
        step = 256
        if last:
            gain = gain_ref[0:1, :]
            gains = jnp.zeros((1, d), F32)
            shifts = jnp.zeros((1, d), F32)
        for r in range(0, seq, step):
            fig = sum(
                dot(
                    dj_scr[r : r + step, k * lanes : (k + 1) * lanes],
                    w_ref[:, k * d + group * lanes : k * d + (group + 1) * lanes],
                    (1, 1),
                )
                for k in range(3)
            )
            if not last:
                fig_ref[r : r + step, :] = fig
                continue
            fig = fig + fig0_ref[r : r + step, :]
            hat, scale = normalize(x_ref[r : r + step, :].astype(F32))
            gains += jnp.sum(fig * hat, axis=0, keepdims=True)
            shifts += jnp.sum(fig, axis=0, keepdims=True)
            grad = hg_ref[r : r + step, :] + norm_back(fig, hat, scale, gain)
            tg_ref[r : r + step, :] = grad.astype(BF)
        if last:
            sums_ref[0:1, :] = gains
            sums_ref[1:2, :] = shifts
            if order.stepped:
                folded = fold_lanes(mine, me, gains, 0, chunk, 128)
                folded += fold_lanes(mine, me, shifts, chunk, chunk, 128)
                block = place_rows(folded, 0, chunk).astype(BF)
                lo_ref[:, 3 * lanes :] = block[: d // 2]
                hi_ref[:, 3 * lanes :] = block[d // 2 :]


def whole(shape):
    return pl.BlockSpec(shape, lambda i: (0,) * len(shape))


def smem():
    return pl.BlockSpec(memory_space=pltpu.SMEM)


def launch(name, kernel, steps, ins, outs, scratch, after=(), mib=8, cost=2 * 10**10, aliases=()):
    n = len(ins)

    def body(*refs):
        kernel(*refs[:n], *refs[n + len(after) :])

    return pl.pallas_call(
        body,
        grid=(steps,),
        in_specs=[s for _, s in ins] + [pl.BlockSpec(memory_space=pl.ANY)] * len(after),
        out_specs=[s for _, s in outs],
        out_shape=[o for o, _ in outs],
        scratch_shapes=scratch,
        compiler_params=pltpu.CompilerParams(
            dimension_semantics=("arbitrary",), vmem_limit_bytes=mib * MIB
        ),
        cost_estimate=pl.CostEstimate(flops=cost, bytes_accessed=0, transcendentals=0),
        input_output_aliases=dict(aliases),
        name=name,
    )(*[a for a, _ in ins], *after)


def out(shape, dtype, spec=None):
    return jax.ShapeDtypeStruct(shape, dtype), whole(shape) if spec is None else spec


def in_hbm(shape, dtype):
    return pltpu.HBM(shape, dtype), whole(shape)


def from_hbm(array):
    return pltpu.with_memory_space_constraint(array, pltpu.HBM), whole(array.shape)


def full(array):
    return array, whole(array.shape)


def by_rows(rows, width, column=0):
    return pl.BlockSpec((rows, width), lambda i: (i, column))


def by_columns(rows, width):
    return pl.BlockSpec((rows, width), lambda i: (0, i))


def by_tiles(shape):
    return pl.BlockSpec((STEP, *shape[1:]), lambda i: (i, 0, 0))


def fixed_columns(rows, width, column):
    return pl.BlockSpec((rows, width), lambda i: (0, column))


def prepare(lens, seq, after=()):
    _, _, window = geometry(seq)
    shape = (seq // TILE, window, 128)
    return launch(
        "prepare",
        functools.partial(prepare_kernel, seq),
        seq // TILE // STEP,
        [(lens, smem())],
        [out(shape, F32, by_tiles(shape))],
        [],
        after,
        cost=0,
    )[0]


def by_blocks(source, width, chunk, blocks):
    group = 128 // chunk
    lane = iota((source.shape[0], 128), 1) // chunk
    columns = []
    for at in range(0, blocks * width, 128):
        column = None
        for k in range(group):
            device, block = (at % width) // chunk + k, at // width
            lanes = (device * blocks + block) * chunk
            piece = source[:, lanes // 128 * 128 : lanes // 128 * 128 + 128]
            shift = (k * chunk - lanes) % 128
            if shift:
                piece = pltpu.roll(piece, shift, 1)
            column = piece if column is None else jnp.where(lane == k, piece, column)
        columns.append(column)
    return columns


def from_blocks(parts, width, chunk, blocks):
    group = 128 // chunk
    lane = iota((parts[0].shape[0], 128), 1) // chunk
    columns = []
    for at in range(0, blocks * width, 128):
        column = None
        for k in range(group):
            device, block = divmod(at // chunk + k, blocks)
            lanes = device * chunk
            piece = parts[block][:, lanes // 128 * 128 : lanes // 128 * 128 + 128]
            shift = (k * chunk - lanes) % 128
            if shift:
                piece = pltpu.roll(piece, shift, 1)
            column = piece if column is None else jnp.where(lane == k, piece, column)
        columns.append(column)
    return columns


def pack_kernel(joint_ref, expand_ref, output_ref, reduce_ref, *refs):
    small, (a_ref, e1_ref, e2_ref) = refs[:6], refs[6:]
    chunk, d = output_ref.shape
    wide = joint_ref.shape[1]

    def line(vectors):
        flat = jnp.concatenate([v[...].reshape(1, v.shape[0]).astype(F32) for v in vectors], axis=1)
        gap = jnp.zeros((1, 128 - flat.shape[1]), F32)
        return jnp.concatenate([flat, gap], axis=1)

    def block(parts):
        gap = jnp.zeros((chunk - len(parts), 128), F32)
        return jnp.concatenate(parts + [gap], axis=0).astype(BF)

    a_ref[:, :wide] = joint_ref[...]
    a_ref[:, wide:] = block([line(small[:2])])
    columns = by_blocks(expand_ref[...].astype(F32), d, chunk, 4)
    for i, column in enumerate(columns):
        target = (e1_ref, e2_ref)[i * 128 // (2 * d)]
        at = i * 128 % (2 * d)
        target[:, at : at + 128] = column.astype(BF)
    for k in range(4):
        target = (e1_ref, e2_ref)[k // 2]
        target[:, (2 + k % 2) * d : (3 + k % 2) * d] = reduce_ref[k * chunk : (k + 1) * chunk, :]
    e1_ref[:, 4 * d : 5 * d] = output_ref[...]
    e1_ref[:, 5 * d :] = block([line(small[2:5]), line(small[5:])])


def pack(joint, expand, output, reduce, small):
    rows, wide = joint.shape
    d = output.shape[1]
    return launch(
        "pack",
        pack_kernel,
        1,
        [from_hbm(a) for a in (joint, expand, output, reduce, *small)],
        [out((rows, wide + 128), BF), out((rows, 5 * d + 128), BF), out((rows, 4 * d), BF)],
        [],
        mib=4,
        cost=0,
    )


def finish_kernel(one_ref, two_ref, expand_ref, reduce_ref, output_ref, *small):
    chunk, d = output_ref.shape
    parts = [one_ref[:, :d], one_ref[:, d : 2 * d], two_ref[:, :d], two_ref[:, d : 2 * d]]
    for i, column in enumerate(from_blocks(parts, d, chunk, 4)):
        expand_ref[:, i * 128 : (i + 1) * 128] = column
    for k in range(4):
        source = (one_ref, two_ref)[k // 2]
        reduce_ref[k * chunk : (k + 1) * chunk, :] = source[:, (2 + k % 2) * d : (3 + k % 2) * d]
    at = two_ref.shape[1] - 128
    output_ref[...] = two_ref[:, at - d : at]
    for k in range(3):
        small[k][...] = two_ref[0:1, at + k * chunk : at + (k + 1) * chunk].reshape(chunk)
    small[3][...] = two_ref[1:2, at : at + 4 * chunk].reshape(4 * chunk)


def finish(one, two, after):
    rows, d = one.shape[0], one.shape[1] // 4
    return launch(
        "finish",
        finish_kernel,
        1,
        [full(one), full(two)],
        [out((rows, 4 * d), F32), out((4 * rows, d), F32), out((rows, d), F32)]
        + [out((rows,), F32)] * 3
        + [out((4 * rows,), F32)],
        [],
        after,
    )


def close_kernel(lanes, before_ref, keep_ref, other_ref, joint_ref, gain_ref, shift_ref):
    total = keep_ref[...].astype(F32) + other_ref[...].astype(F32)
    chunk, d = joint_ref.shape[0], joint_ref.shape[1] // 3
    at = 4 * d
    for k in range(3):
        joint_ref[:, k * d : k * d + lanes] = before_ref[:, at + k * lanes : at + (k + 1) * lanes]
        joint_ref[:, k * d + lanes : (k + 1) * d] = total[:, k * lanes : (k + 1) * lanes]
    gain_ref[...] = total[0:1, 3 * lanes : 3 * lanes + chunk].reshape(chunk)
    shift_ref[...] = total[0:1, 3 * lanes + chunk : 3 * lanes + 2 * chunk].reshape(chunk)


def close(before, pair, d):
    rows = before.shape[0]
    return launch(
        "close",
        functools.partial(close_kernel, d // GROUPS),
        1,
        [full(before), full(pair[0]), full(pair[1])],
        [out((rows, 3 * d), F32)] + [out((rows,), F32)] * 2,
        [],
        cost=0,
    )


def merge_kernel(plan, *refs):
    n = sum(1 if kind == "carry" else 2 * count for kind, count in plan)
    ins, outs = list(refs[:n]), list(refs[n:])
    for kind, count in plan:
        if kind == "carry":
            outs.pop(0)[...] = ins.pop(0)[...]
            continue
        targets = [outs.pop(0) for _ in range(2 if kind == "add" else 1)]
        at = 0
        for _ in range(count):
            first, second = ins.pop(0), ins.pop(0)
            rows, width = first.shape
            columns = slice(at, at + width)
            at += width
            if kind == "join":
                targets[0][:rows, columns] = first[...]
                targets[0][rows:, columns] = second[...]
                continue
            total = first[...].astype(F32) + second[...].astype(F32)
            if kind == "last":
                targets[0][:, columns] = total
                continue
            targets[0][:, columns] = total[: rows // 2].astype(BF)
            targets[1][:, columns] = total[rows // 2 :].astype(BF)


def merge(plan, arrays, after):
    outs = []
    for (kind, _), pairs in zip(plan, arrays, strict=True):
        rows = pairs[0][0].shape[0]
        width = sum(p[0].shape[1] for p in pairs)
        if kind == "carry":
            outs.append(out((rows, width), pairs[0][0].dtype))
        elif kind == "join":
            outs.append(out((2 * rows, width), BF))
        elif kind == "last":
            outs.append(out((rows, width), F32))
        else:
            outs += [out((rows // 2, width), BF)] * 2
    return launch(
        "merge",
        functools.partial(merge_kernel, plan),
        1,
        [full(a) for pairs in arrays for pair in pairs for a in pair],
        outs,
        [],
        after,
        cost=0,
    )


def attend(order, me, group, bias, x, weights, vec, after=()):
    seq, d = x.shape
    lanes = d // GROUPS
    _, total, window = geometry(seq)
    tiles = seq // TILE
    cols = lanes // DIM * TILE
    near, _, far_base = split_levels(seq)
    scratch = [
        pltpu.VMEM((sum(POOL // v.factor for v in near), POOL), BF),
        pltpu.VMEM((total - far_base, seq), BF),
    ]
    ins = [(me, smem()), (bias, by_tiles(bias.shape))]
    if group == 0:
        ins.append(from_hbm(x))
    else:
        ins.append(full(x))
    ins += [full(w) for w in weights]
    outs = [
        out((tiles, window, cols), BF, by_tiles((tiles, window, cols))),
        out((seq, lanes), BF, by_rows(STEP * TILE, lanes)),
        out((seq, lanes), BF),
        out((total, lanes), BF),
        out((total, lanes), BF),
    ]
    if group == 0:
        ins.append(full(vec))
        outs += [out((seq, d), BF), out((d, 3 * d), BF), out((8, d), F32)]
    return launch(
        "attend",
        functools.partial(attend_kernel, order, seq, group),
        tiles // STEP,
        ins,
        outs,
        scratch,
        after,
        cost=2 * 10**10 if group == 0 else 0,
    )


def ffn_scratch(seq, d):
    return [
        pltpu.VMEM((d, 2 * d), BF),
        pltpu.VMEM((d, 2 * d), BF),
        pltpu.VMEM((d, d), BF),
        pltpu.VMEM((1, 2 * d), F32),
        pltpu.VMEM((d, seq), BF),
        pltpu.VMEM((seq, d), BF),
        pltpu.VMEM((seq, d), BF),
        pltpu.VMEM((d, d), BF),
        pltpu.VMEM((8, d), F32),
    ]


def ffn_first(order, me, lens, x, cot, ctx0, ctx1, e1, vec, ebias, after=()):
    seq, d = x.shape
    return launch(
        "ffn_first",
        functools.partial(ffn_kernel, order, 0),
        2,
        [(me, smem()), (lens, smem())]
        + [full(a) for a in (x, cot, ctx0, ctx1, *e1, vec, ebias)],
        [
            out((seq, d), F32),
            out((seq, d), BF),
            out((seq, d), BF),
            out((seq, d), F32),
            out((seq, d), F32),
            out((1, 2 * d), F32),
            out((d // 2, 4 * d), BF),
            out((d // 2, 4 * d), BF),
        ],
        ffn_scratch(seq, d),
        after,
        mib=12,
    )


def ffn_second(order, me, lens, cot, kept, ctx0, ctx1, e1, e2, vec, ebias, after=()):
    seq, d = cot.shape
    width = d + (128 if order.stepped else 0)
    return launch(
        "ffn_second",
        functools.partial(ffn_kernel, order, 1),
        2,
        [(me, smem()), (lens, smem())]
        + [full(a) for a in (cot, *kept, ctx0, ctx1, *e1, *e2, vec, ebias)],
        [
            in_hbm((seq, d), BF),
            out((seq, d), F32),
            out((seq, d), BF),
            out((d // 2, 4 * d), BF),
            out((d // 2, 4 * d), BF),
            out((d // 2, width), BF),
            out((d // 2, width), BF),
            out((8, d), F32),
            out((1, 2 * d), F32),
            out((seq, d), F32),
            out((seq, d), F32),
        ],
        ffn_scratch(seq, d) + [pltpu.VMEM((seq, d), BF)],
        after,
        aliases={3: 1, 6: 9, 7: 10},
        mib=14,
    )


def attend_back(order, me, group, prob, q, cg, kx, vx, first_in, weights, more, after=()):
    seq, d = first_in.shape
    lanes = d // GROUPS
    levels, total, _ = geometry(seq)
    spread = spreading(seq)
    last = group == GROUPS - 1
    extra = (128 if order.stepped else 0) if last else more[0].shape[1]
    ins = [
        (me, smem()),
        (prob, by_tiles(prob.shape)),
        (q, by_rows(STEP * TILE, lanes)),
        (cg, by_rows(STEP * TILE, lanes, group)),
        full(kx),
        full(vx),
        full(first_in),
        full(weights),
        full(jnp.asarray(spread, BF)),
    ]
    ins += [full(a) for a in more]
    outs = [out((d // 2, 3 * lanes + extra), BF)] * 2
    if last:
        outs += [in_hbm((seq, d), BF), out((8, d), F32)]
    else:
        outs.append(out((seq, d), F32))
    return launch(
        "attend_back",
        functools.partial(attend_back_kernel, order, seq, group),
        prob.shape[0] // STEP,
        ins,
        outs,
        [
            pltpu.VMEM((total, lanes), F32),
            pltpu.VMEM((total, lanes), F32),
            pltpu.VMEM((seq, 3 * lanes), BF),
            pltpu.VMEM((d, 3 * lanes), BF),
        ],
        after,
        mib=17,
    )


class Gather:
    def __init__(self, order, value):
        self.order, self.bits, self.have, self.other = order, list(order.bits), value, None
        if not order.stepped:
            half = value.shape[0] // 2
            self.have, self.other, self.bits = value[:half], value[half:], []

    def send(self):
        if self.bits:
            self.other = swap(self.order, self.have, self.bits.pop(0))

    def kind(self):
        return "join", 1

    def pairs(self):
        return [(self.have, self.other)]

    def pair(self):
        return self.have, self.other

    def take(self, outs):
        self.have = outs.pop(0)


class Scatter:
    def __init__(self, order, halves):
        self.order, self.bits, self.halves, self.other = order, order.bits[::-1], halves, None
        self.done = None
        self.beside = []
        if not order.stepped:
            self.done = jnp.concatenate(halves, axis=0).astype(F32)

    def send(self):
        if self.order.stepped:
            self.other = swap(self.order, self.halves[1], self.bits.pop(0))

    def kind(self):
        return "add" if self.bits else "last", 1 + len(self.beside)

    def pairs(self):
        return [(self.halves[0], self.other)] + self.beside

    def absorb(self, chain):
        if self.order.stepped:
            self.beside += chain.pairs()

    def take(self, outs):
        self.beside = []
        if self.bits:
            self.halves = outs.pop(0), outs.pop(0)
        else:
            self.done = outs.pop(0)


def swap(order, value, bit):
    return lax.ppermute(value, AXES, [(i, i ^ bit) for i in range(order.devices)])


def advance(order, chains, after=(), carry=None):
    if not order.stepped:
        return () if carry is None else ((), carry)
    plan = [c.kind() for c in chains]
    arrays = [c.pairs() for c in chains]
    if carry is not None:
        plan.append(("carry", 1))
        arrays.append([(carry,)])
    outs = list(merge(plan, arrays, after))
    marks = tuple(outs)
    if carry is not None:
        carry = outs.pop()
    for c in chains:
        c.take(outs)
        if c.bits:
            c.send()
    return marks[:1] if carry is None else (marks[:1], carry)


def local(order, me, tokens, cotangent, lens, joint_w, output_w, expand_w, reduce_w,
          attn_gain, attn_shift, ffn_gain, ffn_shift, expand_bias, reduce_bias):
    seq, d = tokens.shape
    lanes = d // GROUPS
    rows = joint_w.shape[0]
    ff = expand_w.shape[1]
    vec = jnp.zeros((8, d), F32)
    ebias = jnp.zeros((1, ff), F32)
    if order.stepped:
        small = [attn_gain, attn_shift, ffn_gain, ffn_shift, reduce_bias, expand_bias]
        first, second, third = pack(joint_w, expand_w, output_w, reduce_w, small)
        joint = Gather(order, first)
        e1 = Gather(order, second)
        e2 = Gather(order, third)
    else:
        small = [attn_gain, attn_shift, ffn_gain, ffn_shift, reduce_bias]
        small = [lax.all_gather(v, AXES, tiled=True) for v in small]
        vec = jnp.pad(jnp.stack(small), ((0, 3), (0, 0))).astype(F32)
        ebias = lax.all_gather(expand_bias, AXES, tiled=True)[None].astype(F32)
        e, o, r = [lax.all_gather(w, AXES, axis=0, tiled=True) for w in (expand_w, output_w, reduce_w)]
        r = [r[k * d : (k + 1) * d] for k in range(4)]
        joint = Gather(order, lax.all_gather(joint_w, AXES, axis=0, tiled=True))
        e1 = Gather(order, jnp.concatenate([e[:, : 2 * d], r[0], r[1], o], axis=1))
        e2 = Gather(order, jnp.concatenate([e[:, 2 * d :], r[2], r[3]], axis=1))
    joint.send()
    mark = advance(order, [joint])
    e1.send()
    mark = advance(order, [joint, e1], mark)
    e2.send()
    mark = advance(order, [joint, e1, e2], mark)
    bias = prepare(lens, seq, mark)
    mark = advance(order, [joint, e1, e2], (bias,))
    p0, ctx0, q0, kx0, vx0, first_in, w, gain = attend(order, me, 0, bias, tokens, joint.pair(), vec, mark)
    p1, ctx1, q1, kx1, vx1 = attend(order, me, 1, bias, first_in, (w,), vec, (ctx0,))
    mark = advance(order, [e1, e2], (ctx1,))
    *kept, lo, hi = ffn_first(
        order, me, lens, tokens, cotangent, ctx0, ctx1, e1.pair(), vec, ebias, mark
    )
    t1 = Scatter(order, (lo, hi))
    mark = advance(order, [e2], (lo,))
    t1.send()
    mark = advance(order, [t1], mark)
    mixed, hg, cg, lo, hi, olo, ohi, sums, esum, _, _ = ffn_second(
        order, me, lens, cotangent, kept, ctx0, ctx1, e1.pair(), e2.pair(), vec, ebias, mark
    )
    mark = advance(order, [t1], (cg,))
    t2 = Scatter(order.turned, (lo, hi))
    t2.send()
    lo, hi, fig = attend_back(order, me, 0, p0, q0, cg, kx0, vx0, first_in, w, (olo, ohi), mark)
    mark, hi = advance(order, [t1, t2], (fig,), hi)
    j0 = Scatter(order, (lo, hi))
    j0.send()
    mark = advance(order, [j0], mark)
    lo, hi, token_grad, tail_sums = attend_back(
        order, me, 1, p1, q1, cg, kx1, vx1, first_in, w, (tokens, fig, hg, gain), mark
    )
    mark, hi = advance(order, [t1, t2, j0], (tail_sums,), hi)
    j1 = Scatter(order.turned, (lo, hi))
    j1.send()
    mark = advance(order, [j1], mark)
    t2.absorb(j0)
    mark = advance(order, [t2, t1], mark)
    mark = advance(order, [j1], mark)
    mark = advance(order, [t2], mark)
    mark = advance(order, [j1], mark)
    mark = advance(order, [j1], mark)
    if order.stepped:
        advance(order, [t2], mark)
        expand_grad, reduce_grad, output_grad, *small = finish(t1.done, t2.done, mark)
        joint_grad, *first_small = close(t2.done, j1.pairs()[0], d)
        small = [*first_small, small[0], small[1], small[3], small[2]]
    else:
        parts = []
        for k in range(3):
            parts += [c.done[:, k * lanes : (k + 1) * lanes] for c in (j0, j1)]
        joint_grad = jnp.concatenate(parts, axis=1)
        one, two = t1.done, t2.done
        expand_grad = lax.psum_scatter(
            jnp.concatenate([one[:, : 2 * d], two[:, : 2 * d]], axis=1), AXES, scatter_dimension=0, tiled=True
        )
        reduce_grad = lax.psum_scatter(
            jnp.concatenate([t[:, k * d : (k + 1) * d] for t in (one, two) for k in (2, 3)], axis=0),
            AXES,
            scatter_dimension=0,
            tiled=True,
        )
        output_grad = lax.psum_scatter(j0.done[:, 3 * lanes :], AXES, scatter_dimension=0, tiled=True)
        joint_grad = lax.psum_scatter(joint_grad, AXES, scatter_dimension=0, tiled=True)
        esums = jnp.concatenate([kept[5][0], esum[0]])
        vectors = [tail_sums[0], tail_sums[1], sums[0], sums[1], esums, sums[2]]
        small = [lax.psum_scatter(v, AXES, scatter_dimension=0, tiled=True) for v in vectors]
    return (mixed, token_grad, joint_grad, output_grad, expand_grad, reduce_grad, *small)


def shards(order, *args):
    sub = lax.axis_size("sub")
    me = (lax.axis_index("dp") * sub + lax.axis_index("sub")).astype(jnp.int32).reshape(1)
    return local(order, me, *args)


def solution(mesh):
    order = Order(math.prod(mesh.shape[a] for a in AXES))
    wide = P(AXES, None)
    flat = P(AXES)
    return jax.shard_map(
        functools.partial(shards, order),
        mesh=mesh,
        in_specs=(wide,) * 7 + (flat,) * 6,
        out_specs=(wide,) * 6 + (flat,) * 6,
        check_vma=False,
    )
```

profile of v0, /device:TPU:0, one launch (start us, length us, event | category | flops | bytes accessed | tf_op | source)
XLA Modules:
  0.0 140.0 jit_solution(6783846876733296841)
XLA Ops:
  1.7 4.1 %collective-permute-start = (bf16[16,1664]{1,0:T(8,128)(2,1)S(1)}, bf16[16,1664]{1,0:T(8,128)(2,1)S(1)}, u32[]{:S(2)}, u32[]{:S(2)}) collective-permute-start(bf16[16,1664]{1,0:T(8,128)(2,1)S(1)} %get-tuple-element.101.refs_0_), channel_id=1, source_target_pairs={{0,16},{1,17},{2,18},{3,19},{4,20},{5,21},{6,22},{7,23},{8,24},{9,... | collective-permute-start | bytes 159752 | tf_op jit(solution)/shard_map/ppermute | solution.py:1047
  5.8 2.7 %collective-permute-done.refs_1_ = bf16[16,1664]{1,0:T(8,128)(2,1)S(1)} collective-permute-done((bf16[16,1664]{1,0:T(8,128)(2,1)S(1)}, bf16[16,1664]{1,0:T(8,128)(2,1)S(1)}, u32[]{:S(2)}, u32[]{:S(2)}) %collective-permute-start) | collective-permute-done | bytes 53280 | tf_op jit(solution)/shard_map/ppermute | solution.py:1047
  9.9 3.1 %collective-permute-start.2 = (bf16[16,2688]{1,0:T(8,128)(2,1)S(1)}, bf16[16,2688]{1,0:T(8,128)(2,1)S(1)}, u32[]{:S(2)}, u32[]{:S(2)}) collective-permute-start(bf16[16,2688]{1,0:T(8,128)(2,1)S(1)} %get-tuple-element.102.refs_2_), channel_id=1, source_target_pairs={{0,16},{1,17},{2,18},{3,19},{4,20},{5,21},{6,22},{7,23},{8,24},{9,... | collective-permute-start | bytes 258056 | tf_op jit(solution)/shard_map/ppermute | solution.py:1047
  13.0 3.4 %collective-permute-done.2.refs_3_ = bf16[16,2688]{1,0:T(8,128)(2,1)S(1)} collective-permute-done((bf16[16,2688]{1,0:T(8,128)(2,1)S(1)}, bf16[16,2688]{1,0:T(8,128)(2,1)S(1)}, u32[]{:S(2)}, u32[]{:S(2)}) %collective-permute-start.2) | collective-permute-done | bytes 86048 | tf_op jit(solution)/shard_map/ppermute | solution.py:1047
  18.4 2.0 %collective-permute-start.5 = (bf16[16,2048]{1,0:T(8,128)(2,1)S(1)}, bf16[16,2048]{1,0:T(8,128)(2,1)S(1)}, u32[]{:S(2)}, u32[]{:S(2)}) collective-permute-start(bf16[16,2048]{1,0:T(8,128)(2,1)S(1)} %get-tuple-element.105.refs_4_), channel_id=1, source_target_pairs={{0,16},{1,17},{2,18},{3,19},{4,20},{5,21},{6,22},{7,23},{8,24},{9,... | collective-permute-start | bytes 196616 | tf_op jit(solution)/shard_map/ppermute | solution.py:1047
  20.3 3.3 %collective-permute-done.5.refs_5_ = bf16[16,2048]{1,0:T(8,128)(2,1)S(1)} collective-permute-done((bf16[16,2048]{1,0:T(8,128)(2,1)S(1)}, bf16[16,2048]{1,0:T(8,128)(2,1)S(1)}, u32[]{:S(2)}, u32[]{:S(2)}) %collective-permute-start.5) | collective-permute-done | bytes 65568 | tf_op jit(solution)/shard_map/ppermute | solution.py:1047
  26.3 2.2 %collective-permute-start.8 = (bf16[32,2048]{1,0:T(8,128)(2,1)S(1)}, bf16[32,2048]{1,0:T(8,128)(2,1)S(1)}, u32[]{:S(2)}, u32[]{:S(2)}) collective-permute-start(bf16[32,2048]{1,0:T(8,128)(2,1)S(1)} %get-tuple-element.108.refs_4_), channel_id=1, source_target_pairs={{0,8},{1,9},{2,10},{3,11},{4,12},{5,13},{6,14},{7,15},{8,0},{9,1},... | collective-permute-start | bytes 393224 | tf_op jit(solution)/shard_map/ppermute | solution.py:1047
  29.2 1.9 %prepare.1.refs_6_.refs_1_ = f32[16,288,128]{2,1,0:T(8,128)S(1)} custom-call(s32[1,8]{1,0:T(1,128)S(1)} %copy-done, bf16[128,1664]{1,0:T(8,128)(2,1)S(1)} %get-tuple-element.106.refs_1_.refs_0_), custom_call_target="tpu_custom_call" | custom-call | tf_op jit(solution)/shard_map/prepare/pallas_call | solution.py:598
  36.8 7.1 %attend.2 = (bf16[16,288,256]{2,1,0:T(8,128)(2,1)S(1)}, bf16[1024,256]{1,0:T(8,128)(2,1)S(1)}, bf16[1024,256]{1,0:T(8,128)(2,1)S(1)}, bf16[2192,256]{1,0:T(8,128...) custom-call(s32[1]{0:T(128)} %bitcast.refs_0_, ...), custom_call_target="tpu_custom_call" | custom-call | flops 20000000000 | tf_op jit(solution)/shard_map/attend/pallas_call | solution.py:598
  43.9 4.8 %attend.3 = (bf16[16,288,256]{2,1,0:T(8,128)(2,1)S(1)}, bf16[1024,256]{1,0:T(8,128)(2,1)S(1)}, bf16[1024,256]{1,0:T(8,128)(2,1)S(1)}, bf16[2192,256]{1,0:T(8,128)(2,1)S(1)}, bf16[2192,256]{1,0:T(8,128)(2,1)S(1)}) custom-call(s32[1]{0:T(128)} %bitcast.refs_0_, f32[16,288,128]{2,1,0:T(8,128)S(1)} %prepare.1.refs_6_.refs_1_, ...), custom_call_target="tpu_custom_call" | custom-call | tf_op jit(solution)/shard_map/attend/pallas_call | solution.py:598
  48.8 3.3 %collective-permute-done.10.refs_1_ = bf16[128,2688]{1,0:T(8,128)(2,1)S(1)} collective-permute-done((bf16[128,2688]{1,0:T(8,128)(2,1)S(1)}, bf16[128,2688]{1,0:T(8,128)(2,1)S(1)}, u32[]{:S(2)}, u32[]{:S(2)}) %collective-permute-start.10) | collective-permute-done | bytes 688160 | tf_op jit(solution)/shard_map/ppermute | solution.py:1047
  53.3 2.2 %collective-permute-done.12.refs_7_.refs_12_ = bf16[256,2688]{1,0:T(8,128)(2,1)S(1)} collective-permute-done((bf16[256,2688]{1,0:T(8,128)(2,1)S(1)}, bf16[256,2688]{1,0:T(8,128)(2,1)S(1)}, u32[]{:S(2)}, u32[]{:S(2)}) %collective-permute-start.12) | collective-permute-done | bytes 1376288 | tf_op jit(solution)/shard_map/ppermute | solution.py:1047
  55.5 11.7 %ffn_first.1 = (f32[1024,512]{1,0:T(8,128)S(1)}, bf16[1024,512]{1,0:T(8,128)(2,1)S(1)}, bf16[1024,512]{1,0:T(8,128)(2,1)S(1)}, f32[1024,512]{1,0:T(8,128)S(1)}, ...) custom-call(s32[1]{0:T(128)} %bitcast.refs_0_, ...), custom_call_target="tpu_custom_call" | custom-call | flops 20000000000 | tf_op jit(solution)/shard_map/ffn_first/pallas_call | solution.py:598
  67.9 2.0 %collective-permute-done.15.refs_1_ = bf16[256,2048]{1,0:T(8,128)(2,1)S(1)} collective-permute-done((bf16[256,2048]{1,0:T(8,128)(2,1)S(1)}, bf16[256,2048]{1,0:T(8,128)(2,1)S(1)}, u32[]{:S(2)}, u32[]{:S(2)}) %collective-permute-start.15) | collective-permute-done | bytes 1048608 | tf_op jit(solution)/shard_map/ppermute | solution.py:1047
  71.5 14.6 %ffn_second.1 = (bf16[1024,512]{1,0:T(8,128)(2,1)}, f32[1024,512]{1,0:T(8,128)S(1)}, bf16[1024,512]{1,0:T(8,128)(2,1)S(1)}, bf16[256,2048]{1,0:T(8,128)(2,1)S(1)...) custom-call(s32[1]{0:T(128)} %bitcast.refs_0_, ...), custom_call_target="tpu_custom_call", output_to_operand_aliasing={{1}: (3, {}), {9}: (6, {}), {10}: (7, {})} | custom-call | flops 20000000000 | tf_op jit(solution)/shard_map/ffn_second/pallas_call | solution.py:598
  88.0 6.8 %attend_back.2 = (bf16[256,1408]{1,0:T(8,128)(2,1)S(1)}, bf16[256,1408]{1,0:T(8,128)(2,1)S(1)}, f32[1024,512]{1,0:T(8,128)S(1)}) custom-call(s32[1]{0:T(128)} %bitcast.refs_0_, bf16[16,288,256]{2,1,0:T(8,128)(2,1)S(1)} %get-tuple-element.133.refs_1_, bf16[1024,256]{1,0:T(8,128)(2,1)S(1)} %get-tuple-element.134.refs_2_, ...), custom_call_target="tpu_custom_call" | custom-call | flops 20000000000 | tf_op jit(solution)/shard_map/attend_back/pallas_call | solution.py:598
  95.4 2.6 %collective-permute-start.20 = (bf16[32,2048]{1,0:T(8,128)(2,1)S(1)}, bf16[32,2048]{1,0:T(8,128)(2,1)S(1)}, u32[]{:S(2)}, u32[]{:S(2)}) collective-permute-start(bf16[32,2048]{1,0:T(8,128)(2,1)S(1)} %get-tuple-element.153), channel_id=1, source_target_pairs={{0,8},{1,9},{2,10},{3,11},{4,12},{5,13},{6,14},{7,15},{8,0},{9,1},... | collective-permute-start | bytes 393224 | tf_op jit(solution)/shard_map/ppermute | solution.py:1047
  100.8 8.9 %attend_back.3 = (bf16[256,896]{1,0:T(8,128)(2,1)S(1)}, bf16[256,896]{1,0:T(8,128)(2,1)S(1)}, bf16[1024,512]{1,0:T(8,128)(2,1)}, f32[8,512]{1,0:T(8,128)S(1)}) custom-call(s32[1]{0:T(128)} %bitcast.refs_0_, bf16[16,288,256]{2,1,0:T(8,128)(2,1)S(1)} %get-tuple-element.128.refs_1_, bf16[1024,256]{1,0:T(8,128)(2,1)S(1)} %get-tuple-element.129.refs_2_, ...), custom_call_target="tpu_custom_call" | custom-call | flops 20000000000 | tf_op jit(solution)/shard_map/attend_back/pallas_call | solution.py:598
  109.7 2.2 %collective-permute-done.21.refs_3_ = bf16[128,2048]{1,0:T(8,128)(2,1)S(1)} collective-permute-done((bf16[128,2048]{1,0:T(8,128)(2,1)S(1)}, bf16[128,2048]{1,0:T(8,128)(2,1)S(1)}, u32[]{:S(2)}, u32[]{:S(2)}) %collective-permute-start.21) | collective-permute-done | bytes 524320 | tf_op jit(solution)/shard_map/ppermute | solution.py:1047
  116.9 5.0 %collective-permute-done.25.refs_5_ = bf16[16,2048]{1,0:T(8,128)(2,1)S(1)} collective-permute-done((bf16[16,2048]{1,0:T(8,128)(2,1)S(1)}, bf16[16,2048]{1,0:T(8,128)(2,1)S(1)}, u32[]{:S(2)}, u32[]{:S(2)}) %collective-permute-start.25) | collective-permute-done | bytes 65568 | tf_op jit(solution)/shard_map/ppermute | solution.py:1047
  122.1 2.7 %collective-permute-done.28.refs_1_ = bf16[128,896]{1,0:T(8,128)(2,1)S(1)} collective-permute-done((bf16[128,896]{1,0:T(8,128)(2,1)S(1)}, bf16[128,896]{1,0:T(8,128)(2,1)S(1)}, u32[]{:S(2)}, u32[]{:S(2)}) %collective-permute-start.28) | collective-permute-done | bytes 229408 | tf_op jit(solution)/shard_map/ppermute | solution.py:1047
  126.1 3.0 %collective-permute-done.27.refs_1_ = bf16[32,3456]{1,0:T(8,128)(2,1)S(1)} collective-permute-done((bf16[32,3456]{1,0:T(8,128)(2,1)S(1)}, bf16[32,3456]{1,0:T(8,128)(2,1)S(1)}, u32[]{:S(2)}, u32[]{:S(2)}) %collective-permute-start.27) | collective-permute-done | bytes 221216 | tf_op jit(solution)/shard_map/ppermute | solution.py:1047
  130.1 4.0 %collective-permute-done.31.refs_1_ = bf16[32,896]{1,0:T(8,128)(2,1)S(1)} collective-permute-done((bf16[32,896]{1,0:T(8,128)(2,1)S(1)}, bf16[32,896]{1,0:T(8,128)(2,1)S(1)}, u32[]{:S(2)}, u32[]{:S(2)}) %collective-permute-start.31) | collective-permute-done | bytes 57376 | tf_op jit(solution)/shard_map/ppermute | solution.py:1047
  134.2 2.7 %collective-permute-start.32 = (bf16[16,896]{1,0:T(8,128)(2,1)S(1)}, bf16[16,896]{1,0:T(8,128)(2,1)S(1)}, u32[]{:S(2)}, u32[]{:S(2)}) collective-permute-start(bf16[16,896]{1,0:T(8,128)(2,1)S(1)} %get-tuple-element.178), channel_id=1, source_target_pairs={{0,16},{1,17},{2,18},{3,19},{4,20},{5,21},{6,22},{7,23},{8,24},{9,... | collective-permute-start | bytes 86024 | tf_op jit(solution)/shard_map/ppermute | solution.py:1047
  (82 shorter events, 32.8 us)
Async XLA Ops:
  1.7 6.8 %collective-permute-start = (bf16[16,1664]{1,0:T(8,128)(2,1)S(1)}, bf16[16,1664]{1,0:T(8,128)(2,1)S(1)}, u32[]{:S(2)}, u32[]{:S(2)}) collective-permute-start(bf16[16,1664]{1,0:T(8,128)(2,1)S(1)} %get-tuple-element.101.refs_0_), channel_id=1, source_target_pairs={{0,16},{1,17},{2,18},{3,19},{4,20},{5,21},{6,22},{7,23},{8,24},{9,... | collective-permute-start | bytes 159752 | tf_op jit(solution)/shard_map/ppermute | solution.py:1047
  8.5 7.8 %collective-permute-start.1 = (bf16[32,1664]{1,0:T(8,128)(2,1)S(1)}, bf16[32,1664]{1,0:T(8,128)(2,1)S(1)}, u32[]{:S(2)}, u32[]{:S(2)}) collective-permute-start(bf16[32,1664]{1,0:T(8,128)(2,1)S(1)} %merge.18.refs_0_.refs_4_), channel_id=1, source_target_pairs={{0,8},{1,9},{2,10},{3,11},{4,12},{5,13},{6,14},{7,15},{8,0},{9,1},... | collective-permute-start | bytes 319496 | tf_op jit(solution)/shard_map/ppermute | solution.py:1047
  9.9 6.4 %collective-permute-start.2 = (bf16[16,2688]{1,0:T(8,128)(2,1)S(1)}, bf16[16,2688]{1,0:T(8,128)(2,1)S(1)}, u32[]{:S(2)}, u32[]{:S(2)}) collective-permute-start(bf16[16,2688]{1,0:T(8,128)(2,1)S(1)} %get-tuple-element.102.refs_2_), channel_id=1, source_target_pairs={{0,16},{1,17},{2,18},{3,19},{4,20},{5,21},{6,22},{7,23},{8,24},{9,... | collective-permute-start | bytes 258056 | tf_op jit(solution)/shard_map/ppermute | solution.py:1047
  16.4 7.8 %collective-permute-start.3 = (bf16[64,1664]{1,0:T(8,128)(2,1)S(1)}, bf16[64,1664]{1,0:T(8,128)(2,1)S(1)}, u32[]{:S(2)}, u32[]{:S(2)}) collective-permute-start(bf16[64,1664]{1,0:T(8,128)(2,1)S(1)} %get-tuple-element.103.refs_0_.refs_6_), channel_id=1, source_target_pairs={{0,4},{1,5},{2,6},{3,7},{4,0},{5,1},{6,2},{7,3},{8,12},{9,13},{10,... | collective-permute-start | bytes 638984 | tf_op jit(solution)/shard_map/ppermute | solution.py:1047
  18.1 6.1 %collective-permute-start.4 = (bf16[32,2688]{1,0:T(8,128)(2,1)S(1)}, bf16[32,2688]{1,0:T(8,128)(2,1)S(1)}, u32[]{:S(2)}, u32[]{:S(2)}) collective-permute-start(bf16[32,2688]{1,0:T(8,128)(2,1)S(1)} %get-tuple-element.104.refs_2_), channel_id=1, source_target_pairs={{0,8},{1,9},{2,10},{3,11},{4,12},{5,13},{6,14},{7,15},{8,0},{9,1},... | collective-permute-start | bytes 516104 | tf_op jit(solution)/shard_map/ppermute | solution.py:1047
  18.4 5.3 %collective-permute-start.5 = (bf16[16,2048]{1,0:T(8,128)(2,1)S(1)}, bf16[16,2048]{1,0:T(8,128)(2,1)S(1)}, u32[]{:S(2)}, u32[]{:S(2)}) collective-permute-start(bf16[16,2048]{1,0:T(8,128)(2,1)S(1)} %get-tuple-element.105.refs_4_), channel_id=1, source_target_pairs={{0,16},{1,17},{2,18},{3,19},{4,20},{5,21},{6,22},{7,23},{8,24},{9,... | collective-permute-start | bytes 196616 | tf_op jit(solution)/shard_map/ppermute | solution.py:1047
  24.3 8.8 %collective-permute-start.6 = (bf16[128,1664]{1,0:T(8,128)(2,1)S(1)}, bf16[128,1664]{1,0:T(8,128)(2,1)S(1)}, u32[]{:S(2)}, u32[]{:S(2)}) collective-permute-start(bf16[128,1664]{1,0:T(8,128)(2,1)S(1)} %get-tuple-element.106.refs_1_.refs_0_), channel_id=1, source_target_pairs={{0,2},{1,3},{2,0},{3,1},{4,6},{5,7},{6,4},{7,5},{8,10},{9,11},{10,... | collective-permute-start | bytes 1277960 | tf_op jit(solution)/shard_map/ppermute | solution.py:1047
  25.8 7.2 %collective-permute-start.7 = (bf16[64,2688]{1,0:T(8,128)(2,1)S(1)}, bf16[64,2688]{1,0:T(8,128)(2,1)S(1)}, u32[]{:S(2)}, u32[]{:S(2)}) collective-permute-start(bf16[64,2688]{1,0:T(8,128)(2,1)S(1)} %get-tuple-element.107.refs_2_), channel_id=1, source_target_pairs={{0,4},{1,5},{2,6},{3,7},{4,0},{5,1},{6,2},{7,3},{8,12},{9,13},{10,... | collective-permute-start | bytes 1032200 | tf_op jit(solution)/shard_map/ppermute | solution.py:1047
  26.3 5.2 %collective-permute-start.8 = (bf16[32,2048]{1,0:T(8,128)(2,1)S(1)}, bf16[32,2048]{1,0:T(8,128)(2,1)S(1)}, u32[]{:S(2)}, u32[]{:S(2)}) collective-permute-start(bf16[32,2048]{1,0:T(8,128)(2,1)S(1)} %get-tuple-element.108.refs_4_), channel_id=1, source_target_pairs={{0,8},{1,9},{2,10},{3,11},{4,12},{5,13},{6,14},{7,15},{8,0},{9,1},... | collective-permute-start | bytes 393224 | tf_op jit(solution)/shard_map/ppermute | solution.py:1047
  34.1 14.7 %collective-permute-start.11 = (bf16[64,2048]{1,0:T(8,128)(2,1)S(1)}, bf16[64,2048]{1,0:T(8,128)(2,1)S(1)}, u32[]{:S(2)}, u32[]{:S(2)}) collective-permute-start(bf16[64,2048]{1,0:T(8,128)(2,1)S(1)} %get-tuple-element.115.refs_2_), channel_id=1, source_target_pairs={{0,4},{1,5},{2,6},{3,7},{4,0},{5,1},{6,2},{7,3},{8,12},{9,13},{10,... | collective-permute-start | bytes 786440 | tf_op jit(solution)/shard_map/ppermute | solution.py:1047
  34.6 17.6 %collective-permute-start.10 = (bf16[128,2688]{1,0:T(8,128)(2,1)S(1)}, bf16[128,2688]{1,0:T(8,128)(2,1)S(1)}, u32[]{:S(2)}, u32[]{:S(2)}) collective-permute-start(bf16[128,2688]{1,0:T(8,128)(2,1)S(1)} %get-tuple-element.114.refs_0_), channel_id=1, source_target_pairs={{0,2},{1,3},{2,0},{3,1},{4,6},{5,7},{6,4},{7,5},{8,10},{9,11},{10,... | collective-permute-start | bytes 2064392 | tf_op jit(solution)/shard_map/ppermute | solution.py:1047
  52.3 15.1 %collective-permute-start.13 = (bf16[128,2048]{1,0:T(8,128)(2,1)S(1)}, bf16[128,2048]{1,0:T(8,128)(2,1)S(1)}, u32[]{:S(2)}, u32[]{:S(2)}) collective-permute-start(bf16[128,2048]{1,0:T(8,128)(2,1)S(1)} %get-tuple-element.123.refs_0_), channel_id=1, source_target_pairs={{0,2},{1,3},{2,0},{3,1},{4,6},{5,7},{6,4},{7,5},{8,10},{9,11},{10,... | collective-permute-start | bytes 1572872 | tf_op jit(solution)/shard_map/ppermute | solution.py:1047
  70.2 16.0 %collective-permute-start.16 = (bf16[128,2048]{1,0:T(8,128)(2,1)S(1)}, bf16[128,2048]{1,0:T(8,128)(2,1)S(1)}, u32[]{:S(2)}, u32[]{:S(2)}) collective-permute-start(bf16[128,2048]{1,0:T(8,128)(2,1)S(1)} %get-tuple-element.139), channel_id=1, source_target_pairs={{0,2},{1,3},{2,0},{3,1},{4,6},{5,7},{6,4},{7,5},{8,10},{9,11},{10,... | collective-permute-start | bytes 1572872 | tf_op jit(solution)/shard_map/ppermute | solution.py:1047
  86.1 8.9 %collective-permute-start.18 = (bf16[256,2048]{1,0:T(8,128)(2,1)S(1)}, bf16[256,2048]{1,0:T(8,128)(2,1)S(1)}, u32[]{:S(2)}, u32[]{:S(2)}) collective-permute-start(bf16[256,2048]{1,0:T(8,128)(2,1)S(1)} %get-tuple-element.147), channel_id=1, source_target_pairs={{0,1},{1,0},{2,3},{3,2},{4,5},{5,4},{6,7},{7,6},{8,9},{9,8},{10,11... | collective-permute-start | bytes 3145736 | tf_op jit(solution)/shard_map/ppermute | solution.py:1047
  86.3 8.6 %collective-permute-start.17 = (bf16[64,2048]{1,0:T(8,128)(2,1)S(1)}, bf16[64,2048]{1,0:T(8,128)(2,1)S(1)}, u32[]{:S(2)}, u32[]{:S(2)}) collective-permute-start(bf16[64,2048]{1,0:T(8,128)(2,1)S(1)} %get-tuple-element.145), channel_id=1, source_target_pairs={{0,4},{1,5},{2,6},{3,7},{4,0},{5,1},{6,2},{7,3},{8,12},{9,13},{10,... | collective-permute-start | bytes 786440 | tf_op jit(solution)/shard_map/ppermute | solution.py:1047
  95.4 14.3 %collective-permute-start.20 = (bf16[32,2048]{1,0:T(8,128)(2,1)S(1)}, bf16[32,2048]{1,0:T(8,128)(2,1)S(1)}, u32[]{:S(2)}, u32[]{:S(2)}) collective-permute-start(bf16[32,2048]{1,0:T(8,128)(2,1)S(1)} %get-tuple-element.153), channel_id=1, source_target_pairs={{0,8},{1,9},{2,10},{3,11},{4,12},{5,13},{6,14},{7,15},{8,0},{9,1},... | collective-permute-start | bytes 393224 | tf_op jit(solution)/shard_map/ppermute | solution.py:1047
  98.0 14.0 %collective-permute-start.21 = (bf16[128,2048]{1,0:T(8,128)(2,1)S(1)}, bf16[128,2048]{1,0:T(8,128)(2,1)S(1)}, u32[]{:S(2)}, u32[]{:S(2)}) collective-permute-start(bf16[128,2048]{1,0:T(8,128)(2,1)S(1)} %get-tuple-element.155), channel_id=1, source_target_pairs={{0,4},{1,5},{2,6},{3,7},{4,0},{5,1},{6,2},{7,3},{8,12},{9,13},{10,... | collective-permute-start | bytes 1572872 | tf_op jit(solution)/shard_map/ppermute | solution.py:1047
  99.9 12.1 %collective-permute-start.22 = (bf16[128,1408]{1,0:T(8,128)(2,1)S(1)}, bf16[128,1408]{1,0:T(8,128)(2,1)S(1)}, u32[]{:S(2)}, u32[]{:S(2)}) collective-permute-start(bf16[128,1408]{1,0:T(8,128)(2,1)S(1)} %get-tuple-element.156), channel_id=1, source_target_pairs={{0,2},{1,3},{2,0},{3,1},{4,6},{5,7},{6,4},{7,5},{8,10},{9,11},{10,... | collective-permute-start | bytes 1081352 | tf_op jit(solution)/shard_map/ppermute | solution.py:1047
  112.3 9.6 %collective-permute-start.23 = (bf16[64,2048]{1,0:T(8,128)(2,1)S(1)}, bf16[64,2048]{1,0:T(8,128)(2,1)S(1)}, u32[]{:S(2)}, u32[]{:S(2)}) collective-permute-start(bf16[64,2048]{1,0:T(8,128)(2,1)S(1)} %get-tuple-element.160), channel_id=1, source_target_pairs={{0,2},{1,3},{2,0},{3,1},{4,6},{5,7},{6,4},{7,5},{8,10},{9,11},{10,... | collective-permute-start | bytes 786440 | tf_op jit(solution)/shard_map/ppermute | solution.py:1047
  113.3 8.6 %collective-permute-start.24 = (bf16[64,1408]{1,0:T(8,128)(2,1)S(1)}, bf16[64,1408]{1,0:T(8,128)(2,1)S(1)}, u32[]{:S(2)}, u32[]{:S(2)}) collective-permute-start(bf16[64,1408]{1,0:T(8,128)(2,1)S(1)} %get-tuple-element.162), channel_id=1, source_target_pairs={{0,4},{1,5},{2,6},{3,7},{4,0},{5,1},{6,2},{7,3},{8,12},{9,13},{10,... | collective-permute-start | bytes 540680 | tf_op jit(solution)/shard_map/ppermute | solution.py:1047
  115.1 9.7 %collective-permute-start.28 = (bf16[128,896]{1,0:T(8,128)(2,1)S(1)}, bf16[128,896]{1,0:T(8,128)(2,1)S(1)}, u32[]{:S(2)}, u32[]{:S(2)}) collective-permute-start(bf16[128,896]{1,0:T(8,128)(2,1)S(1)} %get-tuple-element.170), channel_id=1, source_target_pairs={{0,4},{1,5},{2,6},{3,7},{4,0},{5,1},{6,2},{7,3},{8,12},{9,13},{10,... | collective-permute-start | bytes 688136 | tf_op jit(solution)/shard_map/ppermute | solution.py:1047
  116.0 5.9 %collective-permute-start.25 = (bf16[16,2048]{1,0:T(8,128)(2,1)S(1)}, bf16[16,2048]{1,0:T(8,128)(2,1)S(1)}, u32[]{:S(2)}, u32[]{:S(2)}) collective-permute-start(bf16[16,2048]{1,0:T(8,128)(2,1)S(1)} %get-tuple-element.164), channel_id=1, source_target_pairs={{0,16},{1,17},{2,18},{3,19},{4,20},{5,21},{6,22},{7,23},{8,24},{9,... | collective-permute-start | bytes 196616 | tf_op jit(solution)/shard_map/ppermute | solution.py:1047
  122.0 7.1 %collective-permute-start.27 = (bf16[32,3456]{1,0:T(8,128)(2,1)S(1)}, bf16[32,3456]{1,0:T(8,128)(2,1)S(1)}, u32[]{:S(2)}, u32[]{:S(2)}) collective-permute-start(bf16[32,3456]{1,0:T(8,128)(2,1)S(1)} %get-tuple-element.169), channel_id=1, source_target_pairs={{0,8},{1,9},{2,10},{3,11},{4,12},{5,13},{6,14},{7,15},{8,0},{9,1},... | collective-permute-start | bytes 663560 | tf_op jit(solution)/shard_map/ppermute | solution.py:1047
  129.2 7.7 %collective-permute-start.29 = (bf16[16,3456]{1,0:T(8,128)(2,1)S(1)}, bf16[16,3456]{1,0:T(8,128)(2,1)S(1)}, u32[]{:S(2)}, u32[]{:S(2)}) collective-permute-start(bf16[16,3456]{1,0:T(8,128)(2,1)S(1)} %get-tuple-element.173), channel_id=1, source_target_pairs={{0,16},{1,17},{2,18},{3,19},{4,20},{5,21},{6,22},{7,23},{8,24},{9,... | collective-permute-start | bytes 331784 | tf_op jit(solution)/shard_map/ppermute | solution.py:1047
  (14 other events, 56.8 us)
where the time goes:
time: 140 us
  Pallas kernels  61.3 us (44%)
  waiting for transfers between devices  40.2 us (29%)
  starting transfers between devices  36.9 us (26%)
    pallas_call x28, Pallas kernels, launch(): pl.pallas_call(body, grid=(steps,), in_specs=[s for _, s in ins] + [pl.Bl...  61.3 us
    ppermute x33, waiting for transfers between devices, swap(): lax.ppermute(value, AXES, [(i, i ^ bit) for i in range(order.devices)])  40.2 us
    ppermute x33, starting transfers between devices, swap(): lax.ppermute(value, AXES, [(i, i ^ bit) for i in range(order.devices)])  36.9 us
  transfers between devices with their start and end apart: 33, of which 20 were waited for; matrix products, arithmetic and copies ran while one was open for 0% of the time, Pallas kernels for 41%

commit v1 on v0

--- a/solution.py
+++ b/solution.py
@@ -484,8 +484,8 @@
 ):
     last = group == GROUPS - 1
     if last:
-        x_ref, fig0_ref, hg_ref, gain_ref, lo_ref, hi_ref, tg_ref, sums_ref = refs[:8]
-        dk_scr, dv_scr, dj_scr, j_scr = refs[8:]
+        x_ref, fig0_ref, lo_ref, hi_ref, fig_ref, sums_ref = refs[:6]
+        dk_scr, dv_scr, dj_scr, j_scr = refs[6:]
     else:
         olo_ref, ohi_ref, lo_ref, hi_ref, fig_ref = refs[:5]
         dk_scr, dv_scr, dj_scr, j_scr = refs[5:]
@@ -549,7 +549,6 @@
         pack_rows(mine, me, j_scr, (lo_ref, hi_ref), slice(0, 3 * lanes), chunk)
         step = 256
         if last:
-            gain = gain_ref[0:1, :]
             gains = jnp.zeros((1, d), F32)
             shifts = jnp.zeros((1, d), F32)
         for r in range(0, seq, step):
@@ -561,15 +560,14 @@
                 )
                 for k in range(3)
             )
+            if last:
+                fig = fig + fig0_ref[r : r + step, :]
+            fig_ref[r : r + step, :] = fig
             if not last:
-                fig_ref[r : r + step, :] = fig
                 continue
-            fig = fig + fig0_ref[r : r + step, :]
-            hat, scale = normalize(x_ref[r : r + step, :].astype(F32))
+            hat, _ = normalize(x_ref[r : r + step, :].astype(F32))
             gains += jnp.sum(fig * hat, axis=0, keepdims=True)
             shifts += jnp.sum(fig, axis=0, keepdims=True)
-            grad = hg_ref[r : r + step, :] + norm_back(fig, hat, scale, gain)
-            tg_ref[r : r + step, :] = grad.astype(BF)
         if last:
             sums_ref[0:1, :] = gains
             sums_ref[1:2, :] = shifts
@@ -613,10 +611,6 @@
 
 def out(shape, dtype, spec=None):
     return jax.ShapeDtypeStruct(shape, dtype), whole(shape) if spec is None else spec
-
-
-def in_hbm(shape, dtype):
-    return pltpu.HBM(shape, dtype), whole(shape)
 
 
 def from_hbm(array):
@@ -929,7 +923,7 @@
         [(me, smem()), (lens, smem())]
         + [full(a) for a in (cot, *kept, ctx0, ctx1, *e1, *e2, vec, ebias)],
         [
-            in_hbm((seq, d), BF),
+            out((seq, d), BF),
             out((seq, d), F32),
             out((seq, d), BF),
             out((d // 2, 4 * d), BF),
@@ -967,11 +961,9 @@
         full(jnp.asarray(spread, BF)),
     ]
     ins += [full(a) for a in more]
-    outs = [out((d // 2, 3 * lanes + extra), BF)] * 2
+    outs = [out((d // 2, 3 * lanes + extra), BF)] * 2 + [out((seq, d), F32)]
     if last:
-        outs += [in_hbm((seq, d), BF), out((8, d), F32)]
-    else:
-        outs.append(out((seq, d), F32))
+        outs.append(out((8, d), F32))
     return launch(
         "attend_back",
         functools.partial(attend_back_kernel, order, seq, group),
@@ -989,6 +981,29 @@
     )
 
 
+def token_kernel(x_ref, fig_ref, hg_ref, gain_ref, kept_ref, tg_ref, mixed_ref, mark_ref):
+    hat, scale = normalize(x_ref[...].astype(F32))
+    grad = hg_ref[...] + norm_back(fig_ref[...], hat, scale, gain_ref[0:1, :])
+    tg_ref[...] = grad.astype(BF)
+    mixed_ref[...] = kept_ref[...]
+    mark_ref[...] = jnp.zeros_like(mark_ref)
+
+
+def token_grads(x, fig, hidden_grad, gain, kept, after=()):
+    seq, d = x.shape
+    rows = 512
+    return launch(
+        "token_grad",
+        token_kernel,
+        seq // rows,
+        [(a, by_rows(rows, d)) for a in (x, fig, hidden_grad)] + [full(gain), (kept, by_rows(rows, d))],
+        [(pltpu.HBM((seq, d), BF), by_rows(rows, d))] * 2 + [out((8, 128), F32)],
+        [],
+        after,
+        cost=0,
+    )
+
+
 class Gather:
     def __init__(self, order, value):
         self.order, self.bits, self.have, self.other = order, list(order.bits), value, None
@@ -1047,7 +1062,7 @@
     return lax.ppermute(value, AXES, [(i, i ^ bit) for i in range(order.devices)])
 
 
-def advance(order, chains, after=(), carry=None):
+def advance(order, chains, after=(), carry=None, hold=()):
     if not order.stepped:
         return () if carry is None else ((), carry)
     plan = [c.kind() for c in chains]
@@ -1061,9 +1076,16 @@
         carry = outs.pop()
     for c in chains:
         c.take(outs)
-        if c.bits:
+        if c.bits and c not in hold:
             c.send()
     return marks[:1] if carry is None else (marks[:1], carry)
+
+
+def release(order, held, chains, after):
+    mark, high = advance(order, chains, after, held.halves[1])
+    held.halves = held.halves[0], high
+    held.send()
+    return mark
 
 
 def local(order, me, tokens, cotangent, lens, joint_w, output_w, expand_w, reduce_w,
@@ -1115,19 +1137,21 @@
     t2 = Scatter(order.turned, (lo, hi))
     t2.send()
     lo, hi, fig = attend_back(order, me, 0, p0, q0, cg, kx0, vx0, first_in, w, (olo, ohi), mark)
-    mark, hi = advance(order, [t1, t2], (fig,), hi)
+    mark, hi = advance(order, [t1, t2], (fig,), hi, [t1])
     j0 = Scatter(order, (lo, hi))
     j0.send()
-    mark = advance(order, [j0], mark)
-    lo, hi, token_grad, tail_sums = attend_back(
-        order, me, 1, p1, q1, cg, kx1, vx1, first_in, w, (tokens, fig, hg, gain), mark
-    )
-    mark, hi = advance(order, [t1, t2, j0], (tail_sums,), hi)
+    mark = release(order, t1, [j0], mark)
+    lo, hi, fig, tail_sums = attend_back(
+        order, me, 1, p1, q1, cg, kx1, vx1, first_in, w, (tokens, fig), mark
+    )
+    mark, hi = advance(order, [t1, t2, j0], (tail_sums,), hi, [t1, j0])
     j1 = Scatter(order.turned, (lo, hi))
     j1.send()
-    mark = advance(order, [j1], mark)
+    mark = release(order, j0, [j1], mark)
+    t1.send()
+    token_grad, mixed, mark = token_grads(tokens, fig, hg, gain, mixed, mark)
     t2.absorb(j0)
-    mark = advance(order, [t2, t1], mark)
+    mark = advance(order, [t2, t1], (mark,))
     mark = advance(order, [j1], mark)
     mark = advance(order, [t2], mark)
     mark = advance(order, [j1], mark)

time: 140 us -> 139 us (level)
  waiting for transfers between devices: 40.2 us -> 36.8 us
  starting transfers between devices: 36.9 us -> 38.6 us
    ppermute x33, waiting for transfers between devices: 40.2 us -> 36.8 us  [swap(): lax.ppermute(value, AXES, [(i, i ^ bit) for i in range(order.devices)])]
    ppermute x33, starting transfers between devices: 36.9 us -> 38.6 us  [swap(): lax.ppermute(value, AXES, [(i, i ^ bit) for i in range(order.devices)])]
    pallas_call x28 -> x29, Pallas kernels: 61.3 us -> 61.6 us  [launch(): pl.pallas_call(body, grid=(steps,), in_specs=[s for _, s in ins] + [pl.Bl...]
  transfers between devices with their start and end apart: 33 -> 33, of which waited for: 20 -> 22; matrix products, arithmetic and copies ran while one was open for 0% -> 0% of each run, Pallas kernels for 41% -> 42%
where the time goes in v1:
time: 139 us
  Pallas kernels  61.6 us (44%)
  starting transfers between devices  38.6 us (28%)
  waiting for transfers between devices  36.8 us (26%)
    pallas_call x29, Pallas kernels, launch(): pl.pallas_call(body, grid=(steps,), in_specs=[s for _, s in ins] + [pl.Bl...  61.6 us
    ppermute x33, starting transfers between devices, swap(): lax.ppermute(value, AXES, [(i, i ^ bit) for i in range(order.devices)])  38.6 us
    ppermute x33, waiting for transfers between devices, swap(): lax.ppermute(value, AXES, [(i, i ^ bit) for i in range(order.devices)])  36.8 us
  transfers between devices with their start and end apart: 33, of which 22 were waited for; matrix products, arithmetic and copies ran while one was open for 0% of the time, Pallas kernels for 42%

profile of v1, /device:TPU:0, one launch (start us, length us, event | category | flops | bytes accessed | tf_op | source)
XLA Modules:
  0.0 138.6 jit_solution(3970834244141401528)
XLA Ops:
  1.7 4.1 %collective-permute-start = (bf16[16,1664]{1,0:T(8,128)(2,1)S(1)}, bf16[16,1664]{1,0:T(8,128)(2,1)S(1)}, u32[]{:S(2)}, u32[]{:S(2)}) collective-permute-start(bf16[16,1664]{1,0:T(8,128)(2,1)S(1)} %get-tuple-element.106.refs_0_), channel_id=1, source_target_pairs={{0,16},{1,17},{2,18},{3,19},{4,20},{5,21},{6,22},{7,23},{8,24},{9,... | collective-permute-start | bytes 159752 | tf_op jit(solution)/shard_map/ppermute | solution.py:1062
  5.8 2.7 %collective-permute-done.refs_1_ = bf16[16,1664]{1,0:T(8,128)(2,1)S(1)} collective-permute-done((bf16[16,1664]{1,0:T(8,128)(2,1)S(1)}, bf16[16,1664]{1,0:T(8,128)(2,1)S(1)}, u32[]{:S(2)}, u32[]{:S(2)}) %collective-permute-start) | collective-permute-done | bytes 53280 | tf_op jit(solution)/shard_map/ppermute | solution.py:1062
  9.9 3.1 %collective-permute-start.2 = (bf16[16,2688]{1,0:T(8,128)(2,1)S(1)}, bf16[16,2688]{1,0:T(8,128)(2,1)S(1)}, u32[]{:S(2)}, u32[]{:S(2)}) collective-permute-start(bf16[16,2688]{1,0:T(8,128)(2,1)S(1)} %get-tuple-element.107.refs_2_), channel_id=1, source_target_pairs={{0,16},{1,17},{2,18},{3,19},{4,20},{5,21},{6,22},{7,23},{8,24},{9,... | collective-permute-start | bytes 258056 | tf_op jit(solution)/shard_map/ppermute | solution.py:1062
  13.0 3.4 %collective-permute-done.2.refs_3_ = bf16[16,2688]{1,0:T(8,128)(2,1)S(1)} collective-permute-done((bf16[16,2688]{1,0:T(8,128)(2,1)S(1)}, bf16[16,2688]{1,0:T(8,128)(2,1)S(1)}, u32[]{:S(2)}, u32[]{:S(2)}) %collective-permute-start.2) | collective-permute-done | bytes 86048 | tf_op jit(solution)/shard_map/ppermute | solution.py:1062
  18.4 2.0 %collective-permute-start.5 = (bf16[16,2048]{1,0:T(8,128)(2,1)S(1)}, bf16[16,2048]{1,0:T(8,128)(2,1)S(1)}, u32[]{:S(2)}, u32[]{:S(2)}) collective-permute-start(bf16[16,2048]{1,0:T(8,128)(2,1)S(1)} %get-tuple-element.110.refs_4_), channel_id=1, source_target_pairs={{0,16},{1,17},{2,18},{3,19},{4,20},{5,21},{6,22},{7,23},{8,24},{9,... | collective-permute-start | bytes 196616 | tf_op jit(solution)/shard_map/ppermute | solution.py:1062
  20.3 3.3 %collective-permute-done.5.refs_5_ = bf16[16,2048]{1,0:T(8,128)(2,1)S(1)} collective-permute-done((bf16[16,2048]{1,0:T(8,128)(2,1)S(1)}, bf16[16,2048]{1,0:T(8,128)(2,1)S(1)}, u32[]{:S(2)}, u32[]{:S(2)}) %collective-permute-start.5) | collective-permute-done | bytes 65568 | tf_op jit(solution)/shard_map/ppermute | solution.py:1062
  26.3 2.2 %collective-permute-start.8 = (bf16[32,2048]{1,0:T(8,128)(2,1)S(1)}, bf16[32,2048]{1,0:T(8,128)(2,1)S(1)}, u32[]{:S(2)}, u32[]{:S(2)}) collective-permute-start(bf16[32,2048]{1,0:T(8,128)(2,1)S(1)} %get-tuple-element.113.refs_4_), channel_id=1, source_target_pairs={{0,8},{1,9},{2,10},{3,11},{4,12},{5,13},{6,14},{7,15},{8,0},{9,1},... | collective-permute-start | bytes 393224 | tf_op jit(solution)/shard_map/ppermute | solution.py:1062
  29.2 1.9 %prepare.1.refs_6_.refs_1_ = f32[16,288,128]{2,1,0:T(8,128)S(1)} custom-call(s32[1,8]{1,0:T(1,128)S(1)} %copy-done.1, bf16[128,1664]{1,0:T(8,128)(2,1)S(1)} %get-tuple-element.111.refs_1_.refs_0_), custom_call_target="tpu_custom_call" | custom-call | tf_op jit(solution)/shard_map/prepare/pallas_call | solution.py:596
  36.8 7.0 %attend.2 = (bf16[16,288,256]{2,1,0:T(8,128)(2,1)S(1)}, bf16[1024,256]{1,0:T(8,128)(2,1)S(1)}, bf16[1024,256]{1,0:T(8,128)(2,1)S(1)}, bf16[2192,256]{1,0:T(8,128...) custom-call(s32[1]{0:T(128)} %bitcast.refs_0_, ...), custom_call_target="tpu_custom_call" | custom-call | flops 20000000000 | tf_op jit(solution)/shard_map/attend/pallas_call | solution.py:596
  43.8 4.8 %attend.3 = (bf16[16,288,256]{2,1,0:T(8,128)(2,1)S(1)}, bf16[1024,256]{1,0:T(8,128)(2,1)S(1)}, bf16[1024,256]{1,0:T(8,128)(2,1)S(1)}, bf16[2192,256]{1,0:T(8,128)(2,1)S(1)}, bf16[2192,256]{1,0:T(8,128)(2,1)S(1)}) custom-call(s32[1]{0:T(128)} %bitcast.refs_0_, f32[16,288,128]{2,1,0:T(8,128)S(1)} %prepare.1.refs_6_.refs_1_, ...), custom_call_target="tpu_custom_call" | custom-call | tf_op jit(solution)/shard_map/attend/pallas_call | solution.py:596
  48.7 3.5 %collective-permute-done.10.refs_1_ = bf16[128,2688]{1,0:T(8,128)(2,1)S(1)} collective-permute-done((bf16[128,2688]{1,0:T(8,128)(2,1)S(1)}, bf16[128,2688]{1,0:T(8,128)(2,1)S(1)}, u32[]{:S(2)}, u32[]{:S(2)}) %collective-permute-start.10) | collective-permute-done | bytes 688160 | tf_op jit(solution)/shard_map/ppermute | solution.py:1062
  53.3 2.2 %collective-permute-done.12.refs_7_.refs_12_ = bf16[256,2688]{1,0:T(8,128)(2,1)S(1)} collective-permute-done((bf16[256,2688]{1,0:T(8,128)(2,1)S(1)}, bf16[256,2688]{1,0:T(8,128)(2,1)S(1)}, u32[]{:S(2)}, u32[]{:S(2)}) %collective-permute-start.12) | collective-permute-done | bytes 1376288 | tf_op jit(solution)/shard_map/ppermute | solution.py:1062
  55.5 11.7 %ffn_first.1 = (f32[1024,512]{1,0:T(8,128)S(1)}, bf16[1024,512]{1,0:T(8,128)(2,1)S(1)}, bf16[1024,512]{1,0:T(8,128)(2,1)S(1)}, f32[1024,512]{1,0:T(8,128)S(1)}, ...) custom-call(s32[1]{0:T(128)} %bitcast.refs_0_, ...), custom_call_target="tpu_custom_call" | custom-call | flops 20000000000 | tf_op jit(solution)/shard_map/ffn_first/pallas_call | solution.py:596
  67.9 2.0 %collective-permute-done.15.refs_1_ = bf16[256,2048]{1,0:T(8,128)(2,1)S(1)} collective-permute-done((bf16[256,2048]{1,0:T(8,128)(2,1)S(1)}, bf16[256,2048]{1,0:T(8,128)(2,1)S(1)}, u32[]{:S(2)}, u32[]{:S(2)}) %collective-permute-start.15) | collective-permute-done | bytes 1048608 | tf_op jit(solution)/shard_map/ppermute | solution.py:1062
  71.4 14.2 %ffn_second.1 = (bf16[1024,512]{1,0:T(8,128)(2,1)S(1)}, f32[1024,512]{1,0:T(8,128)S(1)}, bf16[1024,512]{1,0:T(8,128)(2,1)S(1)}, bf16[256,2048]{1,0:T(8,128)(2,1)...) custom-call(s32[1]{0:T(128)} %bitcast.refs_0_, ...), custom_call_target="tpu_custom_call", output_to_operand_aliasing={{1}: (3, {}), {9}: (6, {}), {10}: (7, {})} | custom-call | flops 20000000000 | tf_op jit(solution)/shard_map/ffn_second/pallas_call | solution.py:596
  87.6 6.8 %attend_back.2 = (bf16[256,1408]{1,0:T(8,128)(2,1)S(1)}, bf16[256,1408]{1,0:T(8,128)(2,1)S(1)}, f32[1024,512]{1,0:T(8,128)S(1)}) custom-call(s32[1]{0:T(128)} %bitcast.refs_0_, bf16[16,288,256]{2,1,0:T(8,128)(2,1)S(1)} %get-tuple-element.137.refs_1_, bf16[1024,256]{1,0:T(8,128)(2,1)S(1)} %get-tuple-element.138.refs_2_, ...), custom_call_target="tpu_custom_call" | custom-call | flops 20000000000 | tf_op jit(solution)/shard_map/attend_back/pallas_call | solution.py:596
  97.3 2.6 %collective-permute-start.20 = (bf16[32,2048]{1,0:T(8,128)(2,1)S(1)}, bf16[32,2048]{1,0:T(8,128)(2,1)S(1)}, u32[]{:S(2)}, u32[]{:S(2)}) collective-permute-start(bf16[32,2048]{1,0:T(8,128)(2,1)S(1)} %get-tuple-element.160), channel_id=1, source_target_pairs={{0,8},{1,9},{2,10},{3,11},{4,12},{5,13},{6,14},{7,15},{8,0},{9,1},... | collective-permute-start | bytes 393224 | tf_op jit(solution)/shard_map/ppermute | solution.py:1062
  100.8 7.3 %attend_back.3 = (bf16[256,896]{1,0:T(8,128)(2,1)S(1)}, bf16[256,896]{1,0:T(8,128)(2,1)S(1)}, f32[1024,512]{1,0:T(8,128)S(1)}, f32[8,512]{1,0:T(8,128)S(1)}) custom-call(s32[1]{0:T(128)} %bitcast.refs_0_, bf16[16,288,256]{2,1,0:T(8,128)(2,1)S(1)} %get-tuple-element.118.refs_1_, bf16[1024,256]{1,0:T(8,128)(2,1)S(1)} %get-tuple-element.119.refs_2_, ...), custom_call_target="tpu_custom_call" | custom-call | flops 20000000000 | tf_op jit(solution)/shard_map/attend_back/pallas_call | solution.py:596
  115.5 2.4 %token_grad.1 = (bf16[1024,512]{1,0:T(8,128)(2,1)}, bf16[1024,512]{1,0:T(8,128)(2,1)}, f32[8,128]{1,0:T(8,128)S(1)}) custom-call(bf16[1024,512]{1,0:T(8,128)(2,1)S(1)} %copy-done, f32[1024,512]{1,0:T(8,128)S(1)} %get-tuple-element.155.refs_1_, f32[1024,512]{1,0:T(8,128)S(1)} %get-tuple-element.156.refs_2_, f32[8,512]{1,0:T(8,128)S(1)} %get-tuple-element.157.refs_3_, ...), custom_call_target="tpu_custom_call" | custom-call | tf_op jit(solution)/shard_map/token_grad/pallas_call | solution.py:596
  117.9 2.3 %collective-permute-done.26.refs_5_ = bf16[16,2048]{1,0:T(8,128)(2,1)S(1)} collective-permute-done((bf16[16,2048]{1,0:T(8,128)(2,1)S(1)}, bf16[16,2048]{1,0:T(8,128)(2,1)S(1)}, u32[]{:S(2)}, u32[]{:S(2)}) %collective-permute-start.26) | collective-permute-done | bytes 65568 | tf_op jit(solution)/shard_map/ppermute | solution.py:1062
  121.7 2.2 %collective-permute-done.28.refs_1_ = bf16[128,896]{1,0:T(8,128)(2,1)S(1)} collective-permute-done((bf16[128,896]{1,0:T(8,128)(2,1)S(1)}, bf16[128,896]{1,0:T(8,128)(2,1)S(1)}, u32[]{:S(2)}, u32[]{:S(2)}) %collective-permute-start.28) | collective-permute-done | bytes 229408 | tf_op jit(solution)/shard_map/ppermute | solution.py:1062
  128.9 1.8 %collective-permute-start.31 = (bf16[32,896]{1,0:T(8,128)(2,1)S(1)}, bf16[32,896]{1,0:T(8,128)(2,1)S(1)}, u32[]{:S(2)}, u32[]{:S(2)}) collective-permute-start(bf16[32,896]{1,0:T(8,128)(2,1)S(1)} %get-tuple-element.186), channel_id=1, source_target_pairs={{0,8},{1,9},{2,10},{3,11},{4,12},{5,13},{6,14},{7,15},{8,0},{9,1},... | collective-permute-start | bytes 172040 | tf_op jit(solution)/shard_map/ppermute | solution.py:1062
  130.7 2.4 %collective-permute-done.31.refs_1_ = bf16[32,896]{1,0:T(8,128)(2,1)S(1)} collective-permute-done((bf16[32,896]{1,0:T(8,128)(2,1)S(1)}, bf16[32,896]{1,0:T(8,128)(2,1)S(1)}, u32[]{:S(2)}, u32[]{:S(2)}) %collective-permute-start.31) | collective-permute-done | bytes 57376 | tf_op jit(solution)/shard_map/ppermute | solution.py:1062
  135.6 2.4 %collective-permute-done.32.refs_2_ = bf16[16,896]{1,0:T(8,128)(2,1)S(1)} collective-permute-done((bf16[16,896]{1,0:T(8,128)(2,1)S(1)}, bf16[16,896]{1,0:T(8,128)(2,1)S(1)}, u32[]{:S(2)}, u32[]{:S(2)}) %collective-permute-start.32) | collective-permute-done | bytes 28704 | tf_op jit(solution)/shard_map/ppermute | solution.py:1062
  (83 shorter events, 39.6 us)
Async XLA Ops:
  1.7 6.8 %collective-permute-start = (bf16[16,1664]{1,0:T(8,128)(2,1)S(1)}, bf16[16,1664]{1,0:T(8,128)(2,1)S(1)}, u32[]{:S(2)}, u32[]{:S(2)}) collective-permute-start(bf16[16,1664]{1,0:T(8,128)(2,1)S(1)} %get-tuple-element.106.refs_0_), channel_id=1, source_target_pairs={{0,16},{1,17},{2,18},{3,19},{4,20},{5,21},{6,22},{7,23},{8,24},{9,... | collective-permute-start | bytes 159752 | tf_op jit(solution)/shard_map/ppermute | solution.py:1062
  8.5 7.8 %collective-permute-start.1 = (bf16[32,1664]{1,0:T(8,128)(2,1)S(1)}, bf16[32,1664]{1,0:T(8,128)(2,1)S(1)}, u32[]{:S(2)}, u32[]{:S(2)}) collective-permute-start(bf16[32,1664]{1,0:T(8,128)(2,1)S(1)} %merge.18.refs_0_.refs_4_), channel_id=1, source_target_pairs={{0,8},{1,9},{2,10},{3,11},{4,12},{5,13},{6,14},{7,15},{8,0},{9,1},... | collective-permute-start | bytes 319496 | tf_op jit(solution)/shard_map/ppermute | solution.py:1062
  9.9 6.4 %collective-permute-start.2 = (bf16[16,2688]{1,0:T(8,128)(2,1)S(1)}, bf16[16,2688]{1,0:T(8,128)(2,1)S(1)}, u32[]{:S(2)}, u32[]{:S(2)}) collective-permute-start(bf16[16,2688]{1,0:T(8,128)(2,1)S(1)} %get-tuple-element.107.refs_2_), channel_id=1, source_target_pairs={{0,16},{1,17},{2,18},{3,19},{4,20},{5,21},{6,22},{7,23},{8,24},{9,... | collective-permute-start | bytes 258056 | tf_op jit(solution)/shard_map/ppermute | solution.py:1062
  16.4 7.8 %collective-permute-start.3 = (bf16[64,1664]{1,0:T(8,128)(2,1)S(1)}, bf16[64,1664]{1,0:T(8,128)(2,1)S(1)}, u32[]{:S(2)}, u32[]{:S(2)}) collective-permute-start(bf16[64,1664]{1,0:T(8,128)(2,1)S(1)} %get-tuple-element.108.refs_0_.refs_6_), channel_id=1, source_target_pairs={{0,4},{1,5},{2,6},{3,7},{4,0},{5,1},{6,2},{7,3},{8,12},{9,13},{10,... | collective-permute-start | bytes 638984 | tf_op jit(solution)/shard_map/ppermute | solution.py:1062
  18.1 6.1 %collective-permute-start.4 = (bf16[32,2688]{1,0:T(8,128)(2,1)S(1)}, bf16[32,2688]{1,0:T(8,128)(2,1)S(1)}, u32[]{:S(2)}, u32[]{:S(2)}) collective-permute-start(bf16[32,2688]{1,0:T(8,128)(2,1)S(1)} %get-tuple-element.109.refs_2_), channel_id=1, source_target_pairs={{0,8},{1,9},{2,10},{3,11},{4,12},{5,13},{6,14},{7,15},{8,0},{9,1},... | collective-permute-start | bytes 516104 | tf_op jit(solution)/shard_map/ppermute | solution.py:1062
  18.4 5.3 %collective-permute-start.5 = (bf16[16,2048]{1,0:T(8,128)(2,1)S(1)}, bf16[16,2048]{1,0:T(8,128)(2,1)S(1)}, u32[]{:S(2)}, u32[]{:S(2)}) collective-permute-start(bf16[16,2048]{1,0:T(8,128)(2,1)S(1)} %get-tuple-element.110.refs_4_), channel_id=1, source_target_pairs={{0,16},{1,17},{2,18},{3,19},{4,20},{5,21},{6,22},{7,23},{8,24},{9,... | collective-permute-start | bytes 196616 | tf_op jit(solution)/shard_map/ppermute | solution.py:1062
  24.3 8.8 %collective-permute-start.6 = (bf16[128,1664]{1,0:T(8,128)(2,1)S(1)}, bf16[128,1664]{1,0:T(8,128)(2,1)S(1)}, u32[]{:S(2)}, u32[]{:S(2)}) collective-permute-start(bf16[128,1664]{1,0:T(8,128)(2,1)S(1)} %get-tuple-element.111.refs_1_.refs_0_), channel_id=1, source_target_pairs={{0,2},{1,3},{2,0},{3,1},{4,6},{5,7},{6,4},{7,5},{8,10},{9,11},{10,... | collective-permute-start | bytes 1277960 | tf_op jit(solution)/shard_map/ppermute | solution.py:1062
  25.8 7.2 %collective-permute-start.7 = (bf16[64,2688]{1,0:T(8,128)(2,1)S(1)}, bf16[64,2688]{1,0:T(8,128)(2,1)S(1)}, u32[]{:S(2)}, u32[]{:S(2)}) collective-permute-start(bf16[64,2688]{1,0:T(8,128)(2,1)S(1)} %get-tuple-element.112.refs_2_), channel_id=1, source_target_pairs={{0,4},{1,5},{2,6},{3,7},{4,0},{5,1},{6,2},{7,3},{8,12},{9,13},{10,... | collective-permute-start | bytes 1032200 | tf_op jit(solution)/shard_map/ppermute | solution.py:1062
  26.3 5.2 %collective-permute-start.8 = (bf16[32,2048]{1,0:T(8,128)(2,1)S(1)}, bf16[32,2048]{1,0:T(8,128)(2,1)S(1)}, u32[]{:S(2)}, u32[]{:S(2)}) collective-permute-start(bf16[32,2048]{1,0:T(8,128)(2,1)S(1)} %get-tuple-element.113.refs_4_), channel_id=1, source_target_pairs={{0,8},{1,9},{2,10},{3,11},{4,12},{5,13},{6,14},{7,15},{8,0},{9,1},... | collective-permute-start | bytes 393224 | tf_op jit(solution)/shard_map/ppermute | solution.py:1062
  34.1 14.5 %collective-permute-start.11 = (bf16[64,2048]{1,0:T(8,128)(2,1)S(1)}, bf16[64,2048]{1,0:T(8,128)(2,1)S(1)}, u32[]{:S(2)}, u32[]{:S(2)}) collective-permute-start(bf16[64,2048]{1,0:T(8,128)(2,1)S(1)} %get-tuple-element.122.refs_2_), channel_id=1, source_target_pairs={{0,4},{1,5},{2,6},{3,7},{4,0},{5,1},{6,2},{7,3},{8,12},{9,13},{10,... | collective-permute-start | bytes 786440 | tf_op jit(solution)/shard_map/ppermute | solution.py:1062
  34.6 17.6 %collective-permute-start.10 = (bf16[128,2688]{1,0:T(8,128)(2,1)S(1)}, bf16[128,2688]{1,0:T(8,128)(2,1)S(1)}, u32[]{:S(2)}, u32[]{:S(2)}) collective-permute-start(bf16[128,2688]{1,0:T(8,128)(2,1)S(1)} %get-tuple-element.121.refs_0_), channel_id=1, source_target_pairs={{0,2},{1,3},{2,0},{3,1},{4,6},{5,7},{6,4},{7,5},{8,10},{9,11},{10,... | collective-permute-start | bytes 2064392 | tf_op jit(solution)/shard_map/ppermute | solution.py:1062
  52.3 15.1 %collective-permute-start.13 = (bf16[128,2048]{1,0:T(8,128)(2,1)S(1)}, bf16[128,2048]{1,0:T(8,128)(2,1)S(1)}, u32[]{:S(2)}, u32[]{:S(2)}) collective-permute-start(bf16[128,2048]{1,0:T(8,128)(2,1)S(1)} %get-tuple-element.130.refs_0_), channel_id=1, source_target_pairs={{0,2},{1,3},{2,0},{3,1},{4,6},{5,7},{6,4},{7,5},{8,10},{9,11},{10,... | collective-permute-start | bytes 1572872 | tf_op jit(solution)/shard_map/ppermute | solution.py:1062
  70.2 15.6 %collective-permute-start.16 = (bf16[128,2048]{1,0:T(8,128)(2,1)S(1)}, bf16[128,2048]{1,0:T(8,128)(2,1)S(1)}, u32[]{:S(2)}, u32[]{:S(2)}) collective-permute-start(bf16[128,2048]{1,0:T(8,128)(2,1)S(1)} %get-tuple-element.143), channel_id=1, source_target_pairs={{0,2},{1,3},{2,0},{3,1},{4,6},{5,7},{6,4},{7,5},{8,10},{9,11},{10,... | collective-permute-start | bytes 1572872 | tf_op jit(solution)/shard_map/ppermute | solution.py:1062
  85.6 8.9 %collective-permute-start.18 = (bf16[256,2048]{1,0:T(8,128)(2,1)S(1)}, bf16[256,2048]{1,0:T(8,128)(2,1)S(1)}, u32[]{:S(2)}, u32[]{:S(2)}) collective-permute-start(bf16[256,2048]{1,0:T(8,128)(2,1)S(1)} %get-tuple-element.149), channel_id=1, source_target_pairs={{0,1},{1,0},{2,3},{3,2},{4,5},{5,4},{6,7},{7,6},{8,9},{9,8},{10,11... | collective-permute-start | bytes 3145736 | tf_op jit(solution)/shard_map/ppermute | solution.py:1062
  85.9 8.6 %collective-permute-start.17 = (bf16[64,2048]{1,0:T(8,128)(2,1)S(1)}, bf16[64,2048]{1,0:T(8,128)(2,1)S(1)}, u32[]{:S(2)}, u32[]{:S(2)}) collective-permute-start(bf16[64,2048]{1,0:T(8,128)(2,1)S(1)} %get-tuple-element.147), channel_id=1, source_target_pairs={{0,4},{1,5},{2,6},{3,7},{4,0},{5,1},{6,2},{7,3},{8,12},{9,13},{10,... | collective-permute-start | bytes 786440 | tf_op jit(solution)/shard_map/ppermute | solution.py:1062
  95.0 14.3 %collective-permute-start.21 = (bf16[128,2048]{1,0:T(8,128)(2,1)S(1)}, bf16[128,2048]{1,0:T(8,128)(2,1)S(1)}, u32[]{:S(2)}, u32[]{:S(2)}) collective-permute-start(bf16[128,2048]{1,0:T(8,128)(2,1)S(1)} %get-tuple-element.162), channel_id=1, source_target_pairs={{0,4},{1,5},{2,6},{3,7},{4,0},{5,1},{6,2},{7,3},{8,12},{9,13},{10,... | collective-permute-start | bytes 1572872 | tf_op jit(solution)/shard_map/ppermute | solution.py:1062
  97.3 12.0 %collective-permute-start.20 = (bf16[32,2048]{1,0:T(8,128)(2,1)S(1)}, bf16[32,2048]{1,0:T(8,128)(2,1)S(1)}, u32[]{:S(2)}, u32[]{:S(2)}) collective-permute-start(bf16[32,2048]{1,0:T(8,128)(2,1)S(1)} %get-tuple-element.160), channel_id=1, source_target_pairs={{0,8},{1,9},{2,10},{3,11},{4,12},{5,13},{6,14},{7,15},{8,0},{9,1},... | collective-permute-start | bytes 393224 | tf_op jit(solution)/shard_map/ppermute | solution.py:1062
  99.9 10.2 %collective-permute-start.22 = (bf16[128,1408]{1,0:T(8,128)(2,1)S(1)}, bf16[128,1408]{1,0:T(8,128)(2,1)S(1)}, u32[]{:S(2)}, u32[]{:S(2)}) collective-permute-start(bf16[128,1408]{1,0:T(8,128)(2,1)S(1)} %get-tuple-element.163), channel_id=1, source_target_pairs={{0,2},{1,3},{2,0},{3,1},{4,6},{5,7},{6,4},{7,5},{8,10},{9,11},{10,... | collective-permute-start | bytes 1081352 | tf_op jit(solution)/shard_map/ppermute | solution.py:1062
  110.4 9.8 %collective-permute-start.24 = (bf16[64,2048]{1,0:T(8,128)(2,1)S(1)}, bf16[64,2048]{1,0:T(8,128)(2,1)S(1)}, u32[]{:S(2)}, u32[]{:S(2)}) collective-permute-start(bf16[64,2048]{1,0:T(8,128)(2,1)S(1)} %get-tuple-element.173), channel_id=1, source_target_pairs={{0,2},{1,3},{2,0},{3,1},{4,6},{5,7},{6,4},{7,5},{8,10},{9,11},{10,... | collective-permute-start | bytes 786440 | tf_op jit(solution)/shard_map/ppermute | solution.py:1062
  112.3 7.8 %collective-permute-start.25 = (bf16[64,1408]{1,0:T(8,128)(2,1)S(1)}, bf16[64,1408]{1,0:T(8,128)(2,1)S(1)}, u32[]{:S(2)}, u32[]{:S(2)}) collective-permute-start(bf16[64,1408]{1,0:T(8,128)(2,1)S(1)} %get-tuple-element.175), channel_id=1, source_target_pairs={{0,4},{1,5},{2,6},{3,7},{4,0},{5,1},{6,2},{7,3},{8,12},{9,13},{10,... | collective-permute-start | bytes 540680 | tf_op jit(solution)/shard_map/ppermute | solution.py:1062
  114.1 9.8 %collective-permute-start.28 = (bf16[128,896]{1,0:T(8,128)(2,1)S(1)}, bf16[128,896]{1,0:T(8,128)(2,1)S(1)}, u32[]{:S(2)}, u32[]{:S(2)}) collective-permute-start(bf16[128,896]{1,0:T(8,128)(2,1)S(1)} %get-tuple-element.180), channel_id=1, source_target_pairs={{0,4},{1,5},{2,6},{3,7},{4,0},{5,1},{6,2},{7,3},{8,12},{9,13},{10,... | collective-permute-start | bytes 688136 | tf_op jit(solution)/shard_map/ppermute | solution.py:1062
  114.4 5.7 %collective-permute-start.26 = (bf16[16,2048]{1,0:T(8,128)(2,1)S(1)}, bf16[16,2048]{1,0:T(8,128)(2,1)S(1)}, u32[]{:S(2)}, u32[]{:S(2)}) collective-permute-start(bf16[16,2048]{1,0:T(8,128)(2,1)S(1)} %get-tuple-element.176), channel_id=1, source_target_pairs={{0,16},{1,17},{2,18},{3,19},{4,20},{5,21},{6,22},{7,23},{8,24},{9,... | collective-permute-start | bytes 196616 | tf_op jit(solution)/shard_map/ppermute | solution.py:1062
  120.3 6.0 %collective-permute-start.27 = (bf16[32,3456]{1,0:T(8,128)(2,1)S(1)}, bf16[32,3456]{1,0:T(8,128)(2,1)S(1)}, u32[]{:S(2)}, u32[]{:S(2)}) collective-permute-start(bf16[32,3456]{1,0:T(8,128)(2,1)S(1)} %get-tuple-element.179), channel_id=1, source_target_pairs={{0,8},{1,9},{2,10},{3,11},{4,12},{5,13},{6,14},{7,15},{8,0},{9,1},... | collective-permute-start | bytes 663560 | tf_op jit(solution)/shard_map/ppermute | solution.py:1062
  126.4 8.2 %collective-permute-start.29 = (bf16[16,3456]{1,0:T(8,128)(2,1)S(1)}, bf16[16,3456]{1,0:T(8,128)(2,1)S(1)}, u32[]{:S(2)}, u32[]{:S(2)}) collective-permute-start(bf16[16,3456]{1,0:T(8,128)(2,1)S(1)} %get-tuple-element.183), channel_id=1, source_target_pairs={{0,16},{1,17},{2,18},{3,19},{4,20},{5,21},{6,22},{7,23},{8,24},{9,... | collective-permute-start | bytes 331784 | tf_op jit(solution)/shard_map/ppermute | solution.py:1062
  (14 other events, 53.8 us)

commit v2 on v1

--- a/solution.py
+++ b/solution.py
@@ -280,7 +280,13 @@
                 shift = spread_lanes(order, me, (lo_ref, hi_ref), tail, 0, chunk, chunk, d)
             else:
                 gain, shift = vec_ref[0:1, :], vec_ref[1:2, :]
-            gain_ref[...] = jnp.broadcast_to(gain, gain_ref.shape)
+            gain_ref[0:1, :] = gain
+            for k in range(7):
+                if order.stepped:
+                    row, at = (1, k * chunk) if k < 3 else (2, (k - 3) * chunk)
+                    gain_ref[k + 1 : k + 2, :] = spread_lanes(order, me, (lo_ref, hi_ref), tail, row, at, chunk, d)
+                else:
+                    gain_ref[k + 1 : k + 2, :] = vec_ref[k + 2 : k + 3, :]
         kx_ref[...] = jnp.zeros_like(kx_ref)
         vx_ref[...] = jnp.zeros_like(vx_ref)
         step = 256
@@ -366,12 +372,6 @@
     shared = (lo1_ref, hi1_ref)
     turned = order.turned
     half = ctx0_ref.shape[1]
-    tail = slice(5 * d, 5 * d + 128)
-
-    def bias_of(block, at):
-        if order.stepped:
-            return spread_lanes(order, me, shared, tail, 1, block * chunk, chunk, d)
-        return ebias_ref[:, at : at + d]
 
     def live_rows(span):
         return live_column(lens_ref, span.start, rows).astype(F32)
@@ -406,26 +406,15 @@
         unpack_rows(order, me, own, slice(wide, 2 * wide), wr_scr, chunk)
         unpack_rows(order, me, shared, slice(2 * wide, 2 * wide + d), wo_scr, chunk)
         for k in range(2):
-            block = 2 * part + k
-            eb_scr[:, k * d : (k + 1) * d] = bias_of(block, block * d)
+            block = 4 + 2 * part + k
+            eb_scr[:, k * d : (k + 1) * d] = vec_ref[block : block + 1, :]
+        vec_scr[0:1, :] = vec_ref[1:2, :]
+        vec_scr[1:2, :] = vec_ref[2:3, :] if first else vec_ref[3:4, :]
         if first:
-            if order.stepped:
-                gain = spread_lanes(order, me, shared, tail, 0, 0, chunk, d)
-                shift = spread_lanes(order, me, shared, tail, 0, chunk, chunk, d)
-            else:
-                gain, shift = vec_ref[2:3, :], vec_ref[3:4, :]
-            vec_scr[0:1, :] = gain
-            vec_scr[1:2, :] = shift
             mix_ref[...] = jnp.zeros_like(mix_ref)
             sg_ref[...] = jnp.zeros_like(sg_ref)
         else:
             in_scr[...] = in_ref[...].T
-            if order.stepped:
-                vec_scr[0:1, :] = spread_lanes(order, me, shared, tail, 0, 0, chunk, d)
-                vec_scr[1:2, :] = spread_lanes(order, me, shared, tail, 0, 2 * chunk, chunk, d)
-            else:
-                vec_scr[0:1, :] = vec_ref[2:3, :]
-                vec_scr[1:2, :] = vec_ref[4:5, :]
             sums_ref[...] = jnp.zeros_like(sums_ref)
         if first:
             for r in range(0, seq, rows):
@@ -703,7 +692,7 @@
         return jnp.concatenate(parts + [gap], axis=0).astype(BF)
 
     a_ref[:, :wide] = joint_ref[...]
-    a_ref[:, wide:] = block([line(small[:2])])
+    a_ref[:, wide:] = block([line(small[:2]), line(small[2:5]), line(small[5:])])
     columns = by_blocks(expand_ref[...].astype(F32), d, chunk, 4)
     for i, column in enumerate(columns):
         target = (e1_ref, e2_ref)[i * 128 // (2 * d)]
@@ -713,7 +702,6 @@
         target = (e1_ref, e2_ref)[k // 2]
         target[:, (2 + k % 2) * d : (3 + k % 2) * d] = reduce_ref[k * chunk : (k + 1) * chunk, :]
     e1_ref[:, 4 * d : 5 * d] = output_ref[...]
-    e1_ref[:, 5 * d :] = block([line(small[2:5]), line(small[5:])])
 
 
 def pack(joint, expand, output, reduce, small):
@@ -724,7 +712,7 @@
         pack_kernel,
         1,
         [from_hbm(a) for a in (joint, expand, output, reduce, *small)],
-        [out((rows, wide + 128), BF), out((rows, 5 * d + 128), BF), out((rows, 4 * d), BF)],
+        [out((rows, wide + 128), BF), out((rows, 5 * d), BF), out((rows, 4 * d), BF)],
         [],
         mib=4,
         cost=0,
@@ -1094,7 +1082,7 @@
     lanes = d // GROUPS
     rows = joint_w.shape[0]
     ff = expand_w.shape[1]
-    vec = jnp.zeros((8, d), F32)
+    vec = jnp.zeros((16, d), F32)
     ebias = jnp.zeros((1, ff), F32)
     if order.stepped:
         small = [attn_gain, attn_shift, ffn_gain, ffn_shift, reduce_bias, expand_bias]
@@ -1105,8 +1093,8 @@
     else:
         small = [attn_gain, attn_shift, ffn_gain, ffn_shift, reduce_bias]
         small = [lax.all_gather(v, AXES, tiled=True) for v in small]
-        vec = jnp.pad(jnp.stack(small), ((0, 3), (0, 0))).astype(F32)
-        ebias = lax.all_gather(expand_bias, AXES, tiled=True)[None].astype(F32)
+        small += list(lax.all_gather(expand_bias, AXES, tiled=True).reshape(4, d))
+        vec = jnp.pad(jnp.stack(small), ((0, 7), (0, 0))).astype(F32)
         e, o, r = [lax.all_gather(w, AXES, axis=0, tiled=True) for w in (expand_w, output_w, reduce_w)]
         r = [r[k * d : (k + 1) * d] for k in range(4)]
         joint = Gather(order, lax.all_gather(joint_w, AXES, axis=0, tiled=True))
@@ -1124,14 +1112,14 @@
     p1, ctx1, q1, kx1, vx1 = attend(order, me, 1, bias, first_in, (w,), vec, (ctx0,))
     mark = advance(order, [e1, e2], (ctx1,))
     *kept, lo, hi = ffn_first(
-        order, me, lens, tokens, cotangent, ctx0, ctx1, e1.pair(), vec, ebias, mark
+        order, me, lens, tokens, cotangent, ctx0, ctx1, e1.pair(), gain, ebias, mark
     )
     t1 = Scatter(order, (lo, hi))
     mark = advance(order, [e2], (lo,))
     t1.send()
     mark = advance(order, [t1], mark)
     mixed, hg, cg, lo, hi, olo, ohi, sums, esum, _, _ = ffn_second(
-        order, me, lens, cotangent, kept, ctx0, ctx1, e1.pair(), e2.pair(), vec, ebias, mark
+        order, me, lens, cotangent, kept, ctx0, ctx1, e1.pair(), e2.pair(), gain, ebias, mark
     )
     mark = advance(order, [t1], (cg,))
     t2 = Scatter(order.turned, (lo, hi))

time: 139 us -> 137 us (0.986)
  waiting for transfers between devices: 36.8 us -> 34.7 us
    ppermute x33, waiting for transfers between devices: 36.8 us -> 34.7 us  [swap(): lax.ppermute(value, AXES, [(i, i ^ bit) for i in range(order.devices)])]
  transfers between devices with their start and end apart: 33 -> 33, of which waited for: 22 -> 22; matrix products, arithmetic and copies ran while one was open for 0% -> 0% of each run, Pallas kernels for 42% -> 43%
where the time goes in v2:
time: 137 us
  Pallas kernels  62 us (45%)
  starting transfers between devices  38.7 us (28%)
  waiting for transfers between devices  34.7 us (25%)
    pallas_call x29, Pallas kernels, launch(): pl.pallas_call(body, grid=(steps,), in_specs=[s for _, s in ins] + [pl.Bl...  62 us
    ppermute x33, starting transfers between devices, swap(): lax.ppermute(value, AXES, [(i, i ^ bit) for i in range(order.devices)])  38.7 us
    ppermute x33, waiting for transfers between devices, swap(): lax.ppermute(value, AXES, [(i, i ^ bit) for i in range(order.devices)])  34.7 us
  transfers between devices with their start and end apart: 33, of which 22 were waited for; matrix products, arithmetic and copies ran while one was open for 0% of the time, Pallas kernels for 43%

profile of v2, /device:TPU:0, one launch (start us, length us, event | category | flops | bytes accessed | tf_op | source)
XLA Modules:
  0.0 136.9 jit_solution(10906284119434866259)
XLA Ops:
  1.7 4.1 %collective-permute-start = (bf16[16,1664]{1,0:T(8,128)(2,1)S(1)}, bf16[16,1664]{1,0:T(8,128)(2,1)S(1)}, u32[]{:S(2)}, u32[]{:S(2)}) collective-permute-start(bf16[16,1664]{1,0:T(8,128)(2,1)S(1)} %get-tuple-element.106.refs_0_), channel_id=1, source_target_pairs={{0,16},{1,17},{2,18},{3,19},{4,20},{5,21},{6,22},{7,23},{8,24},{9,... | collective-permute-start | bytes 159752 | tf_op jit(solution)/shard_map/ppermute | solution.py:1050
  5.8 2.7 %collective-permute-done.refs_1_ = bf16[16,1664]{1,0:T(8,128)(2,1)S(1)} collective-permute-done((bf16[16,1664]{1,0:T(8,128)(2,1)S(1)}, bf16[16,1664]{1,0:T(8,128)(2,1)S(1)}, u32[]{:S(2)}, u32[]{:S(2)}) %collective-permute-start) | collective-permute-done | bytes 53280 | tf_op jit(solution)/shard_map/ppermute | solution.py:1050
  9.9 3.1 %collective-permute-start.2 = (bf16[16,2560]{1,0:T(8,128)(2,1)S(1)}, bf16[16,2560]{1,0:T(8,128)(2,1)S(1)}, u32[]{:S(2)}, u32[]{:S(2)}) collective-permute-start(bf16[16,2560]{1,0:T(8,128)(2,1)S(1)} %get-tuple-element.107.refs_2_), channel_id=1, source_target_pairs={{0,16},{1,17},{2,18},{3,19},{4,20},{5,21},{6,22},{7,23},{8,24},{9,... | collective-permute-start | bytes 245768 | tf_op jit(solution)/shard_map/ppermute | solution.py:1050
  13.0 3.3 %collective-permute-done.2.refs_3_ = bf16[16,2560]{1,0:T(8,128)(2,1)S(1)} collective-permute-done((bf16[16,2560]{1,0:T(8,128)(2,1)S(1)}, bf16[16,2560]{1,0:T(8,128)(2,1)S(1)}, u32[]{:S(2)}, u32[]{:S(2)}) %collective-permute-start.2) | collective-permute-done | bytes 81952 | tf_op jit(solution)/shard_map/ppermute | solution.py:1050
  18.3 2.0 %collective-permute-start.5 = (bf16[16,2048]{1,0:T(8,128)(2,1)S(1)}, bf16[16,2048]{1,0:T(8,128)(2,1)S(1)}, u32[]{:S(2)}, u32[]{:S(2)}) collective-permute-start(bf16[16,2048]{1,0:T(8,128)(2,1)S(1)} %get-tuple-element.110.refs_4_), channel_id=1, source_target_pairs={{0,16},{1,17},{2,18},{3,19},{4,20},{5,21},{6,22},{7,23},{8,24},{9,... | collective-permute-start | bytes 196616 | tf_op jit(solution)/shard_map/ppermute | solution.py:1050
  20.3 3.3 %collective-permute-done.5.refs_5_ = bf16[16,2048]{1,0:T(8,128)(2,1)S(1)} collective-permute-done((bf16[16,2048]{1,0:T(8,128)(2,1)S(1)}, bf16[16,2048]{1,0:T(8,128)(2,1)S(1)}, u32[]{:S(2)}, u32[]{:S(2)}) %collective-permute-start.5) | collective-permute-done | bytes 65568 | tf_op jit(solution)/shard_map/ppermute | solution.py:1050
  26.1 2.3 %collective-permute-start.8 = (bf16[32,2048]{1,0:T(8,128)(2,1)S(1)}, bf16[32,2048]{1,0:T(8,128)(2,1)S(1)}, u32[]{:S(2)}, u32[]{:S(2)}) collective-permute-start(bf16[32,2048]{1,0:T(8,128)(2,1)S(1)} %get-tuple-element.113.refs_4_), channel_id=1, source_target_pairs={{0,8},{1,9},{2,10},{3,11},{4,12},{5,13},{6,14},{7,15},{8,0},{9,1},... | collective-permute-start | bytes 393224 | tf_op jit(solution)/shard_map/ppermute | solution.py:1050
  29.1 1.9 %prepare.1.refs_6_.refs_1_ = f32[16,288,128]{2,1,0:T(8,128)S(1)} custom-call(s32[1,8]{1,0:T(1,128)S(1)} %copy-done.1, bf16[128,1664]{1,0:T(8,128)(2,1)S(1)} %get-tuple-element.111.refs_1_.refs_0_), custom_call_target="tpu_custom_call" | custom-call | tf_op jit(solution)/shard_map/prepare/pallas_call | solution.py:585
  36.4 7.8 %attend.2 = (bf16[16,288,256]{2,1,0:T(8,128)(2,1)S(1)}, bf16[1024,256]{1,0:T(8,128)(2,1)S(1)}, bf16[1024,256]{1,0:T(8,128)(2,1)S(1)}, bf16[2192,256]{1,0:T(8,128...) custom-call(s32[1]{0:T(128)} %bitcast.refs_0_, ...), custom_call_target="tpu_custom_call" | custom-call | flops 20000000000 | tf_op jit(solution)/shard_map/attend/pallas_call | solution.py:585
  44.2 4.8 %attend.3 = (bf16[16,288,256]{2,1,0:T(8,128)(2,1)S(1)}, bf16[1024,256]{1,0:T(8,128)(2,1)S(1)}, bf16[1024,256]{1,0:T(8,128)(2,1)S(1)}, bf16[2192,256]{1,0:T(8,128)(2,1)S(1)}, bf16[2192,256]{1,0:T(8,128)(2,1)S(1)}) custom-call(s32[1]{0:T(128)} %bitcast.refs_0_, f32[16,288,128]{2,1,0:T(8,128)S(1)} %prepare.1.refs_6_.refs_1_, ...), custom_call_target="tpu_custom_call" | custom-call | tf_op jit(solution)/shard_map/attend/pallas_call | solution.py:585
  49.1 2.2 %collective-permute-done.10.refs_1_ = bf16[128,2560]{1,0:T(8,128)(2,1)S(1)} collective-permute-done((bf16[128,2560]{1,0:T(8,128)(2,1)S(1)}, bf16[128,2560]{1,0:T(8,128)(2,1)S(1)}, u32[]{:S(2)}, u32[]{:S(2)}) %collective-permute-start.10) | collective-permute-done | bytes 655392 | tf_op jit(solution)/shard_map/ppermute | solution.py:1050
  52.4 2.1 %collective-permute-done.12.refs_7_.refs_12_ = bf16[256,2560]{1,0:T(8,128)(2,1)S(1)} collective-permute-done((bf16[256,2560]{1,0:T(8,128)(2,1)S(1)}, bf16[256,2560]{1,0:T(8,128)(2,1)S(1)}, u32[]{:S(2)}, u32[]{:S(2)}) %collective-permute-start.12) | collective-permute-done | bytes 1310752 | tf_op jit(solution)/shard_map/ppermute | solution.py:1050
  54.5 11.3 %ffn_first.1 = (f32[1024,512]{1,0:T(8,128)S(1)}, bf16[1024,512]{1,0:T(8,128)(2,1)S(1)}, bf16[1024,512]{1,0:T(8,128)(2,1)S(1)}, f32[1024,512]{1,0:T(8,128)S(1)}, ...) custom-call(s32[1]{0:T(128)} %bitcast.refs_0_, ...), custom_call_target="tpu_custom_call" | custom-call | flops 20000000000 | tf_op jit(solution)/shard_map/ffn_first/pallas_call | solution.py:585
  66.6 2.0 %collective-permute-done.15.refs_1_ = bf16[256,2048]{1,0:T(8,128)(2,1)S(1)} collective-permute-done((bf16[256,2048]{1,0:T(8,128)(2,1)S(1)}, bf16[256,2048]{1,0:T(8,128)(2,1)S(1)}, u32[]{:S(2)}, u32[]{:S(2)}) %collective-permute-start.15) | collective-permute-done | bytes 1048608 | tf_op jit(solution)/shard_map/ppermute | solution.py:1050
  70.1 13.7 %ffn_second.1 = (bf16[1024,512]{1,0:T(8,128)(2,1)S(1)}, f32[1024,512]{1,0:T(8,128)S(1)}, bf16[1024,512]{1,0:T(8,128)(2,1)S(1)}, bf16[256,2048]{1,0:T(8,128)(2,1)...) custom-call(s32[1]{0:T(128)} %bitcast.refs_0_, ...), custom_call_target="tpu_custom_call", output_to_operand_aliasing={{1}: (3, {}), {9}: (6, {}), {10}: (7, {})} | custom-call | flops 20000000000 | tf_op jit(solution)/shard_map/ffn_second/pallas_call | solution.py:585
  85.4 7.1 %attend_back.2 = (bf16[256,1408]{1,0:T(8,128)(2,1)S(1)}, bf16[256,1408]{1,0:T(8,128)(2,1)S(1)}, f32[1024,512]{1,0:T(8,128)S(1)}) custom-call(s32[1]{0:T(128)} %bitcast.refs_0_, bf16[16,288,256]{2,1,0:T(8,128)(2,1)S(1)} %get-tuple-element.138.refs_1_, bf16[1024,256]{1,0:T(8,128)(2,1)S(1)} %get-tuple-element.139.refs_2_, ...), custom_call_target="tpu_custom_call" | custom-call | flops 20000000000 | tf_op jit(solution)/shard_map/attend_back/pallas_call | solution.py:585
  95.5 2.7 %collective-permute-start.20 = (bf16[32,2048]{1,0:T(8,128)(2,1)S(1)}, bf16[32,2048]{1,0:T(8,128)(2,1)S(1)}, u32[]{:S(2)}, u32[]{:S(2)}) collective-permute-start(bf16[32,2048]{1,0:T(8,128)(2,1)S(1)} %get-tuple-element.160), channel_id=1, source_target_pairs={{0,8},{1,9},{2,10},{3,11},{4,12},{5,13},{6,14},{7,15},{8,0},{9,1},... | collective-permute-start | bytes 393224 | tf_op jit(solution)/shard_map/ppermute | solution.py:1050
  99.3 7.4 %attend_back.3 = (bf16[256,896]{1,0:T(8,128)(2,1)S(1)}, bf16[256,896]{1,0:T(8,128)(2,1)S(1)}, f32[1024,512]{1,0:T(8,128)S(1)}, f32[8,512]{1,0:T(8,128)S(1)}) custom-call(s32[1]{0:T(128)} %bitcast.refs_0_, bf16[16,288,256]{2,1,0:T(8,128)(2,1)S(1)} %get-tuple-element.118.refs_1_, bf16[1024,256]{1,0:T(8,128)(2,1)S(1)} %get-tuple-element.119.refs_2_, ...), custom_call_target="tpu_custom_call" | custom-call | flops 20000000000 | tf_op jit(solution)/shard_map/attend_back/pallas_call | solution.py:585
  113.6 2.4 %token_grad.1 = (bf16[1024,512]{1,0:T(8,128)(2,1)}, bf16[1024,512]{1,0:T(8,128)(2,1)}, f32[8,128]{1,0:T(8,128)S(1)}) custom-call(bf16[1024,512]{1,0:T(8,128)(2,1)S(1)} %copy-done, f32[1024,512]{1,0:T(8,128)S(1)} %get-tuple-element.156.refs_1_, f32[1024,512]{1,0:T(8,128)S(1)} %get-tuple-element.157.refs_2_, ...), custom_call_target="tpu_custom_call" | custom-call | tf_op jit(solution)/shard_map/token_grad/pallas_call | solution.py:585
  116.0 2.4 %collective-permute-done.26.refs_5_ = bf16[16,2048]{1,0:T(8,128)(2,1)S(1)} collective-permute-done((bf16[16,2048]{1,0:T(8,128)(2,1)S(1)}, bf16[16,2048]{1,0:T(8,128)(2,1)S(1)}, u32[]{:S(2)}, u32[]{:S(2)}) %collective-permute-start.26) | collective-permute-done | bytes 65568 | tf_op jit(solution)/shard_map/ppermute | solution.py:1050
  120.1 2.2 %collective-permute-done.28.refs_1_ = bf16[128,896]{1,0:T(8,128)(2,1)S(1)} collective-permute-done((bf16[128,896]{1,0:T(8,128)(2,1)S(1)}, bf16[128,896]{1,0:T(8,128)(2,1)S(1)}, u32[]{:S(2)}, u32[]{:S(2)}) %collective-permute-start.28) | collective-permute-done | bytes 229408 | tf_op jit(solution)/shard_map/ppermute | solution.py:1050
  127.2 1.8 %collective-permute-start.31 = (bf16[32,896]{1,0:T(8,128)(2,1)S(1)}, bf16[32,896]{1,0:T(8,128)(2,1)S(1)}, u32[]{:S(2)}, u32[]{:S(2)}) collective-permute-start(bf16[32,896]{1,0:T(8,128)(2,1)S(1)} %get-tuple-element.186), channel_id=1, source_target_pairs={{0,8},{1,9},{2,10},{3,11},{4,12},{5,13},{6,14},{7,15},{8,0},{9,1},... | collective-permute-start | bytes 172040 | tf_op jit(solution)/shard_map/ppermute | solution.py:1050
  129.0 2.4 %collective-permute-done.31.refs_1_ = bf16[32,896]{1,0:T(8,128)(2,1)S(1)} collective-permute-done((bf16[32,896]{1,0:T(8,128)(2,1)S(1)}, bf16[32,896]{1,0:T(8,128)(2,1)S(1)}, u32[]{:S(2)}, u32[]{:S(2)}) %collective-permute-start.31) | collective-permute-done | bytes 57376 | tf_op jit(solution)/shard_map/ppermute | solution.py:1050
  133.9 2.4 %collective-permute-done.32.refs_2_ = bf16[16,896]{1,0:T(8,128)(2,1)S(1)} collective-permute-done((bf16[16,896]{1,0:T(8,128)(2,1)S(1)}, bf16[16,896]{1,0:T(8,128)(2,1)S(1)}, u32[]{:S(2)}, u32[]{:S(2)}) %collective-permute-start.32) | collective-permute-done | bytes 28704 | tf_op jit(solution)/shard_map/ppermute | solution.py:1050
  (83 shorter events, 38.7 us)
Async XLA Ops:
  1.7 6.8 %collective-permute-start = (bf16[16,1664]{1,0:T(8,128)(2,1)S(1)}, bf16[16,1664]{1,0:T(8,128)(2,1)S(1)}, u32[]{:S(2)}, u32[]{:S(2)}) collective-permute-start(bf16[16,1664]{1,0:T(8,128)(2,1)S(1)} %get-tuple-element.106.refs_0_), channel_id=1, source_target_pairs={{0,16},{1,17},{2,18},{3,19},{4,20},{5,21},{6,22},{7,23},{8,24},{9,... | collective-permute-start | bytes 159752 | tf_op jit(solution)/shard_map/ppermute | solution.py:1050
  8.5 7.8 %collective-permute-start.1 = (bf16[32,1664]{1,0:T(8,128)(2,1)S(1)}, bf16[32,1664]{1,0:T(8,128)(2,1)S(1)}, u32[]{:S(2)}, u32[]{:S(2)}) collective-permute-start(bf16[32,1664]{1,0:T(8,128)(2,1)S(1)} %merge.18.refs_0_.refs_4_), channel_id=1, source_target_pairs={{0,8},{1,9},{2,10},{3,11},{4,12},{5,13},{6,14},{7,15},{8,0},{9,1},... | collective-permute-start | bytes 319496 | tf_op jit(solution)/shard_map/ppermute | solution.py:1050
  9.9 6.3 %collective-permute-start.2 = (bf16[16,2560]{1,0:T(8,128)(2,1)S(1)}, bf16[16,2560]{1,0:T(8,128)(2,1)S(1)}, u32[]{:S(2)}, u32[]{:S(2)}) collective-permute-start(bf16[16,2560]{1,0:T(8,128)(2,1)S(1)} %get-tuple-element.107.refs_2_), channel_id=1, source_target_pairs={{0,16},{1,17},{2,18},{3,19},{4,20},{5,21},{6,22},{7,23},{8,24},{9,... | collective-permute-start | bytes 245768 | tf_op jit(solution)/shard_map/ppermute | solution.py:1050
  16.3 7.6 %collective-permute-start.3 = (bf16[64,1664]{1,0:T(8,128)(2,1)S(1)}, bf16[64,1664]{1,0:T(8,128)(2,1)S(1)}, u32[]{:S(2)}, u32[]{:S(2)}) collective-permute-start(bf16[64,1664]{1,0:T(8,128)(2,1)S(1)} %get-tuple-element.108.refs_0_.refs_6_), channel_id=1, source_target_pairs={{0,4},{1,5},{2,6},{3,7},{4,0},{5,1},{6,2},{7,3},{8,12},{9,13},{10,... | collective-permute-start | bytes 638984 | tf_op jit(solution)/shard_map/ppermute | solution.py:1050
  17.9 6.0 %collective-permute-start.4 = (bf16[32,2560]{1,0:T(8,128)(2,1)S(1)}, bf16[32,2560]{1,0:T(8,128)(2,1)S(1)}, u32[]{:S(2)}, u32[]{:S(2)}) collective-permute-start(bf16[32,2560]{1,0:T(8,128)(2,1)S(1)} %get-tuple-element.109.refs_2_), channel_id=1, source_target_pairs={{0,8},{1,9},{2,10},{3,11},{4,12},{5,13},{6,14},{7,15},{8,0},{9,1},... | collective-permute-start | bytes 491528 | tf_op jit(solution)/shard_map/ppermute | solution.py:1050
  18.3 5.3 %collective-permute-start.5 = (bf16[16,2048]{1,0:T(8,128)(2,1)S(1)}, bf16[16,2048]{1,0:T(8,128)(2,1)S(1)}, u32[]{:S(2)}, u32[]{:S(2)}) collective-permute-start(bf16[16,2048]{1,0:T(8,128)(2,1)S(1)} %get-tuple-element.110.refs_4_), channel_id=1, source_target_pairs={{0,16},{1,17},{2,18},{3,19},{4,20},{5,21},{6,22},{7,23},{8,24},{9,... | collective-permute-start | bytes 196616 | tf_op jit(solution)/shard_map/ppermute | solution.py:1050
  24.0 8.7 %collective-permute-start.6 = (bf16[128,1664]{1,0:T(8,128)(2,1)S(1)}, bf16[128,1664]{1,0:T(8,128)(2,1)S(1)}, u32[]{:S(2)}, u32[]{:S(2)}) collective-permute-start(bf16[128,1664]{1,0:T(8,128)(2,1)S(1)} %get-tuple-element.111.refs_1_.refs_0_), channel_id=1, source_target_pairs={{0,2},{1,3},{2,0},{3,1},{4,6},{5,7},{6,4},{7,5},{8,10},{9,11},{10,... | collective-permute-start | bytes 1277960 | tf_op jit(solution)/shard_map/ppermute | solution.py:1050
  25.6 7.1 %collective-permute-start.7 = (bf16[64,2560]{1,0:T(8,128)(2,1)S(1)}, bf16[64,2560]{1,0:T(8,128)(2,1)S(1)}, u32[]{:S(2)}, u32[]{:S(2)}) collective-permute-start(bf16[64,2560]{1,0:T(8,128)(2,1)S(1)} %get-tuple-element.112.refs_2_), channel_id=1, source_target_pairs={{0,4},{1,5},{2,6},{3,7},{4,0},{5,1},{6,2},{7,3},{8,12},{9,13},{10,... | collective-permute-start | bytes 983048 | tf_op jit(solution)/shard_map/ppermute | solution.py:1050
  26.1 5.3 %collective-permute-start.8 = (bf16[32,2048]{1,0:T(8,128)(2,1)S(1)}, bf16[32,2048]{1,0:T(8,128)(2,1)S(1)}, u32[]{:S(2)}, u32[]{:S(2)}) collective-permute-start(bf16[32,2048]{1,0:T(8,128)(2,1)S(1)} %get-tuple-element.113.refs_4_), channel_id=1, source_target_pairs={{0,8},{1,9},{2,10},{3,11},{4,12},{5,13},{6,14},{7,15},{8,0},{9,1},... | collective-permute-start | bytes 393224 | tf_op jit(solution)/shard_map/ppermute | solution.py:1050
  33.7 15.4 %collective-permute-start.11 = (bf16[64,2048]{1,0:T(8,128)(2,1)S(1)}, bf16[64,2048]{1,0:T(8,128)(2,1)S(1)}, u32[]{:S(2)}, u32[]{:S(2)}) collective-permute-start(bf16[64,2048]{1,0:T(8,128)(2,1)S(1)} %get-tuple-element.122.refs_2_), channel_id=1, source_target_pairs={{0,4},{1,5},{2,6},{3,7},{4,0},{5,1},{6,2},{7,3},{8,12},{9,13},{10,... | collective-permute-start | bytes 786440 | tf_op jit(solution)/shard_map/ppermute | solution.py:1050
  34.4 16.9 %collective-permute-start.10 = (bf16[128,2560]{1,0:T(8,128)(2,1)S(1)}, bf16[128,2560]{1,0:T(8,128)(2,1)S(1)}, u32[]{:S(2)}, u32[]{:S(2)}) collective-permute-start(bf16[128,2560]{1,0:T(8,128)(2,1)S(1)} %get-tuple-element.121.refs_0_), channel_id=1, source_target_pairs={{0,2},{1,3},{2,0},{3,1},{4,6},{5,7},{6,4},{7,5},{8,10},{9,11},{10,... | collective-permute-start | bytes 1966088 | tf_op jit(solution)/shard_map/ppermute | solution.py:1050
  51.5 14.6 %collective-permute-start.13 = (bf16[128,2048]{1,0:T(8,128)(2,1)S(1)}, bf16[128,2048]{1,0:T(8,128)(2,1)S(1)}, u32[]{:S(2)}, u32[]{:S(2)}) collective-permute-start(bf16[128,2048]{1,0:T(8,128)(2,1)S(1)} %get-tuple-element.131.refs_0_), channel_id=1, source_target_pairs={{0,2},{1,3},{2,0},{3,1},{4,6},{5,7},{6,4},{7,5},{8,10},{9,11},{10,... | collective-permute-start | bytes 1572872 | tf_op jit(solution)/shard_map/ppermute | solution.py:1050
  68.8 15.1 %collective-permute-start.16 = (bf16[128,2048]{1,0:T(8,128)(2,1)S(1)}, bf16[128,2048]{1,0:T(8,128)(2,1)S(1)}, u32[]{:S(2)}, u32[]{:S(2)}) collective-permute-start(bf16[128,2048]{1,0:T(8,128)(2,1)S(1)} %get-tuple-element.144), channel_id=1, source_target_pairs={{0,2},{1,3},{2,0},{3,1},{4,6},{5,7},{6,4},{7,5},{8,10},{9,11},{10,... | collective-permute-start | bytes 1572872 | tf_op jit(solution)/shard_map/ppermute | solution.py:1050
  83.8 8.9 %collective-permute-start.18 = (bf16[256,2048]{1,0:T(8,128)(2,1)S(1)}, bf16[256,2048]{1,0:T(8,128)(2,1)S(1)}, u32[]{:S(2)}, u32[]{:S(2)}) collective-permute-start(bf16[256,2048]{1,0:T(8,128)(2,1)S(1)} %get-tuple-element.150), channel_id=1, source_target_pairs={{0,1},{1,0},{2,3},{3,2},{4,5},{5,4},{6,7},{7,6},{8,9},{9,8},{10,11... | collective-permute-start | bytes 3145736 | tf_op jit(solution)/shard_map/ppermute | solution.py:1050
  84.1 8.7 %collective-permute-start.17 = (bf16[64,2048]{1,0:T(8,128)(2,1)S(1)}, bf16[64,2048]{1,0:T(8,128)(2,1)S(1)}, u32[]{:S(2)}, u32[]{:S(2)}) collective-permute-start(bf16[64,2048]{1,0:T(8,128)(2,1)S(1)} %get-tuple-element.148), channel_id=1, source_target_pairs={{0,4},{1,5},{2,6},{3,7},{4,0},{5,1},{6,2},{7,3},{8,12},{9,13},{10,... | collective-permute-start | bytes 786440 | tf_op jit(solution)/shard_map/ppermute | solution.py:1050
  93.1 14.3 %collective-permute-start.21 = (bf16[128,2048]{1,0:T(8,128)(2,1)S(1)}, bf16[128,2048]{1,0:T(8,128)(2,1)S(1)}, u32[]{:S(2)}, u32[]{:S(2)}) collective-permute-start(bf16[128,2048]{1,0:T(8,128)(2,1)S(1)} %get-tuple-element.162), channel_id=1, source_target_pairs={{0,4},{1,5},{2,6},{3,7},{4,0},{5,1},{6,2},{7,3},{8,12},{9,13},{10,... | collective-permute-start | bytes 1572872 | tf_op jit(solution)/shard_map/ppermute | solution.py:1050
  95.5 12.0 %collective-permute-start.20 = (bf16[32,2048]{1,0:T(8,128)(2,1)S(1)}, bf16[32,2048]{1,0:T(8,128)(2,1)S(1)}, u32[]{:S(2)}, u32[]{:S(2)}) collective-permute-start(bf16[32,2048]{1,0:T(8,128)(2,1)S(1)} %get-tuple-element.160), channel_id=1, source_target_pairs={{0,8},{1,9},{2,10},{3,11},{4,12},{5,13},{6,14},{7,15},{8,0},{9,1},... | collective-permute-start | bytes 393224 | tf_op jit(solution)/shard_map/ppermute | solution.py:1050
  98.2 10.2 %collective-permute-start.22 = (bf16[128,1408]{1,0:T(8,128)(2,1)S(1)}, bf16[128,1408]{1,0:T(8,128)(2,1)S(1)}, u32[]{:S(2)}, u32[]{:S(2)}) collective-permute-start(bf16[128,1408]{1,0:T(8,128)(2,1)S(1)} %get-tuple-element.163), channel_id=1, source_target_pairs={{0,2},{1,3},{2,0},{3,1},{4,6},{5,7},{6,4},{7,5},{8,10},{9,11},{10,... | collective-permute-start | bytes 1081352 | tf_op jit(solution)/shard_map/ppermute | solution.py:1050
  108.7 9.7 %collective-permute-start.24 = (bf16[64,2048]{1,0:T(8,128)(2,1)S(1)}, bf16[64,2048]{1,0:T(8,128)(2,1)S(1)}, u32[]{:S(2)}, u32[]{:S(2)}) collective-permute-start(bf16[64,2048]{1,0:T(8,128)(2,1)S(1)} %get-tuple-element.173), channel_id=1, source_target_pairs={{0,2},{1,3},{2,0},{3,1},{4,6},{5,7},{6,4},{7,5},{8,10},{9,11},{10,... | collective-permute-start | bytes 786440 | tf_op jit(solution)/shard_map/ppermute | solution.py:1050
  110.7 7.8 %collective-permute-start.25 = (bf16[64,1408]{1,0:T(8,128)(2,1)S(1)}, bf16[64,1408]{1,0:T(8,128)(2,1)S(1)}, u32[]{:S(2)}, u32[]{:S(2)}) collective-permute-start(bf16[64,1408]{1,0:T(8,128)(2,1)S(1)} %get-tuple-element.175), channel_id=1, source_target_pairs={{0,4},{1,5},{2,6},{3,7},{4,0},{5,1},{6,2},{7,3},{8,12},{9,13},{10,... | collective-permute-start | bytes 540680 | tf_op jit(solution)/shard_map/ppermute | solution.py:1050
  112.2 10.1 %collective-permute-start.28 = (bf16[128,896]{1,0:T(8,128)(2,1)S(1)}, bf16[128,896]{1,0:T(8,128)(2,1)S(1)}, u32[]{:S(2)}, u32[]{:S(2)}) collective-permute-start(bf16[128,896]{1,0:T(8,128)(2,1)S(1)} %get-tuple-element.180), channel_id=1, source_target_pairs={{0,4},{1,5},{2,6},{3,7},{4,0},{5,1},{6,2},{7,3},{8,12},{9,13},{10,... | collective-permute-start | bytes 688136 | tf_op jit(solution)/shard_map/ppermute | solution.py:1050
  112.8 5.7 %collective-permute-start.26 = (bf16[16,2048]{1,0:T(8,128)(2,1)S(1)}, bf16[16,2048]{1,0:T(8,128)(2,1)S(1)}, u32[]{:S(2)}, u32[]{:S(2)}) collective-permute-start(bf16[16,2048]{1,0:T(8,128)(2,1)S(1)} %get-tuple-element.176), channel_id=1, source_target_pairs={{0,16},{1,17},{2,18},{3,19},{4,20},{5,21},{6,22},{7,23},{8,24},{9,... | collective-permute-start | bytes 196616 | tf_op jit(solution)/shard_map/ppermute | solution.py:1050
  118.6 6.1 %collective-permute-start.27 = (bf16[32,3456]{1,0:T(8,128)(2,1)S(1)}, bf16[32,3456]{1,0:T(8,128)(2,1)S(1)}, u32[]{:S(2)}, u32[]{:S(2)}) collective-permute-start(bf16[32,3456]{1,0:T(8,128)(2,1)S(1)} %get-tuple-element.179), channel_id=1, source_target_pairs={{0,8},{1,9},{2,10},{3,11},{4,12},{5,13},{6,14},{7,15},{8,0},{9,1},... | collective-permute-start | bytes 663560 | tf_op jit(solution)/shard_map/ppermute | solution.py:1050
  124.7 8.2 %collective-permute-start.29 = (bf16[16,3456]{1,0:T(8,128)(2,1)S(1)}, bf16[16,3456]{1,0:T(8,128)(2,1)S(1)}, u32[]{:S(2)}, u32[]{:S(2)}) collective-permute-start(bf16[16,3456]{1,0:T(8,128)(2,1)S(1)} %get-tuple-element.183), channel_id=1, source_target_pairs={{0,16},{1,17},{2,18},{3,19},{4,20},{5,21},{6,22},{7,23},{8,24},{9,... | collective-permute-start | bytes 331784 | tf_op jit(solution)/shard_map/ppermute | solution.py:1050
  (14 other events, 49.2 us)
